TPU v7x, 32 devices: a whole 2x2x4 slice. The times are simulated.
32 devices in a mesh: atoms: 8 (over z, x), feat: 4 (over y, core).
Axes of the slice: x: 2, y: 2, z: 4, core: 2. Of those that a mesh axis runs over, the one named last changes fastest.
Arguments:
- features: bfloat16 [256, 8192], P(None, 'atoms'), may hold values from -18 to 18
- vectors: bfloat16 [3, 256, 8192], P(None, None, 'atoms'), may hold values from -18 to 18
- positions: float32 [3, 8192], P(None, 'atoms'), may hold values from -0.3 to 4.65
- atom_mask: int32 [8192], P('atoms'), may hold values from 0 to 1, as said below
- neighbours: int32 [32, 8192], P(None, 'atoms'), may hold values from 0 to 8191, as said below
- ln_gain: float32 [256], replicated, may hold values from 0.5 to 1.5
- ln_bias: float32 [256], replicated, may hold values from -3 to 3
- w_query: bfloat16 [256, 256], P(None, 'feat'), may hold values from -0.375 to 0.375
- w_key: bfloat16 [256, 256], P(None, 'feat'), may hold values from -0.375 to 0.375
- w_value: bfloat16 [3, 256, 256], P(None, None, 'feat'), may hold values from -0.375 to 0.375
- w_vector: bfloat16 [3, 256, 256], P(None, None, 'feat'), may hold values from -0.375 to 0.375
- w_output: bfloat16 [3, 256, 256], P(None, None, 'feat'), may hold values from -0.1875 to 0.1875
- w_key_filter: bfloat16 [64, 256], P(None, 'feat'), may hold values from -4 to 4
- w_value_filter: bfloat16 [3, 64, 256], P(None, None, 'feat'), may hold values from -4 to 4
- cot_features: bfloat16 [256, 8192], P('feat', 'atoms'), may hold values from -6 to 6
- cot_vectors: bfloat16 [3, 256, 8192], P(None, 'feat', 'atoms'), may hold values from -6 to 6
Outputs:
- layer_features: bfloat16 [256, 8192], P('feat', 'atoms')
- layer_vectors: bfloat16 [3, 256, 8192], P(None, 'feat', 'atoms')
- grad_features: float32 [256, 8192], P('feat', 'atoms')
- grad_vectors: float32 [3, 256, 8192], P(None, 'feat', 'atoms')
- grad_positions: float32 [3, 8192], P(None, 'atoms')
- grad_ln_gain: float32 [256], P('feat')
- grad_ln_bias: float32 [256], P('feat')
- grad_w_query: float32 [256, 256], P(None, 'feat')
- grad_w_key: float32 [256, 256], P(None, 'feat')
- grad_w_value: float32 [3, 256, 256], P(None, None, 'feat')
- grad_w_vector: float32 [3, 256, 256], P(None, None, 'feat')
- grad_w_output: float32 [3, 256, 256], P(None, None, 'feat')
- grad_w_key_filter: float32 [64, 256], P(None, 'feat')
- grad_w_value_filter: float32 [3, 64, 256], P(None, None, 'feat')
- stream_rms: float32 [4], replicated
Inputs may be any that keep to these rules, and one draw needn't show every extreme that they name: `atom_mask`: atoms come in blocks of 29 consecutive slots, one molecule each; in each block the first slots are real atoms (mask 1) and the rest padding; the last block, and every block that holds atoms of two consecutive runs of 1024 atoms, is all real. `neighbours`: for a real atom, row 0 is the next real atom of its block, cyclically, and the other rows are real atoms of its own block; every row of a padding slot is the slot itself.
All inputs are finite; a program needn't handle non-finite values.
Results may differ from a plain program's by a relative error of at most 0.011.
Values may be sent and summed in bfloat16 or wider, within the bound.
No kernel may reach another device: no remote copies, remote signals or barrier semaphores. Data moves between devices by JAX's collectives and lax.ppermute only.
A program may use at most 64 MiB of HBM per device.

v0:
```python
import functools
import math

import jax
import jax.numpy as jnp
from jax import lax
from jax.experimental import pallas as pl
from jax.experimental.pallas import tpu as pltpu
from jax.sharding import PartitionSpec as P

H = 256
HEADS = 8
HEAD = H // HEADS
R = 64
MOL = 29
HALO = 32
CUTOFF = 5.0
EPSILON = 1e-05
F32 = jnp.float32
BF16 = jnp.bfloat16

LANE_GROUPS = 2
ROW_GROUPS = 3
SPAN = 5
OFFSETS = 14
STEPS = SPAN + OFFSETS
SUB = 16
LANES = 128

W01, W2V2, C01, C2_COUNT, POS, QK, V0_COUNT, V12, VEC01, VEC2 = range(10)
GROUP_ROWS = 352
EARLY = 9 * R + R // 2
LATE = 2 * R + R // 2
EXTRAS = 16


BLOCK = 8
WINDOW = 256


def block_list(molecules, rows):
    full, rest = divmod(molecules, BLOCK)
    wide = ROW_GROUPS * BLOCK
    out = [(n * wide, wide, BLOCK) for n in range(full)]
    if rows > full * wide:
        out.append((full * wide, rows - full * wide, rest))
    return out


def row_parts(shape, axis, size):
    row = lax.broadcasted_iota(jnp.int32, shape, axis)
    group = jnp.zeros(shape, jnp.int32)
    for g in range(1, ROW_GROUPS):
        group = jnp.where(row >= g * size, g, group)
    return group, row - group * size, row < ROW_GROUPS * size


def set_distances(target, width, size):
    for r in range(LANE_GROUPS):

        def step(t, _, r=r):
            group, molecule, held = row_parts((width, WINDOW), 0, size)
            spot = t + SPAN * (LANE_GROUPS * group + r)
            spot = jnp.where(spot >= MOL, spot - MOL, spot)
            lane = lax.broadcasted_iota(jnp.int32, (width, WINDOW), 1)
            value = jnp.where(held, molecule * MOL + spot - lane, -(10**6))
            target[r, pl.ds(t * width, width), :] = value
            return 0

        lax.fori_loop(0, STEPS, step, 0)


def windows(blocks, distances, start, tall):
    for n, (first, width, size) in enumerate(blocks):
        atom = start + n * BLOCK * MOL
        base = jnp.minimum(atom // SUB * SUB, tall - WINDOW)
        base = pl.multiple_of(base, SUB)
        chosen = distances[0] if size == BLOCK else distances[1]
        ones = [jnp.where(chosen[r] == base - atom, 1.0, 0.0).astype(BF16) for r in (0, 1)]
        yield first, width, pl.ds(base, WINDOW), ones


def spread(source, lanes, stage, blocks, distances, start):
    for first, width, here, ones in windows(blocks, distances, start, source.shape[0]):
        given = source[here, lanes]
        a, b = dot(ones[0], given), dot(ones[1], given)
        low = lax.broadcasted_iota(jnp.int32, (a.shape[0], LANES), 1) < R
        for n in range(a.shape[1] // LANES):
            left, right = a[:, n * LANES : (n + 1) * LANES], b[:, n * LANES : (n + 1) * LANES]
            one = jnp.where(low, left, pltpu.roll(right, R, 1))
            two = jnp.where(low, pltpu.roll(left, R, 1), right)
            stage[2 * n, :, first : first + width] = one.reshape(STEPS, width, LANES)
            stage[2 * n + 1, :, first : first + width] = two.reshape(STEPS, width, LANES)


def spread_positions(source, lanes, targets, blocks, distances, start):
    row = lax.broadcasted_iota(jnp.int32, (LANES, 3 * LANES), 0)
    lane = lax.broadcasted_iota(jnp.int32, (LANES, 3 * LANES), 1)
    axis = jnp.where(lane >= 2 * LANES, 2, jnp.where(lane >= LANES, 1, 0))
    mine = (row >= 3 * axis) & (row < 3 * axis + 3)
    low = lane - axis * LANES < R
    wide = [jnp.where(mine & (low == (r == 0)), 1.0, 0.0).astype(BF16) for r in (0, 1)]
    for first, width, here, ones in windows(blocks, distances, start, source.shape[0]):
        given = source[here, lanes]
        total = 0.0
        for r in (0, 1):
            total = total + dot(dot(ones[r], given).astype(BF16), wide[r])
        for d, target in enumerate(targets):
            value = total[:, d * LANES : (d + 1) * LANES]
            target[:, first : first + width] = value.reshape(STEPS, width, LANES)


def collect(sources, target, blocks, distances, start):
    target[...] = jnp.zeros(target.shape, F32)
    units = []
    for first, width, here, ones in windows(blocks, distances, start, target.shape[0]):
        units.append((first, width, here, ones))
    at = 0
    while at < len(units):
        group = units[at : at + 2] if units[at][0] % SUB == 0 and at + 1 < len(units) else None
        if group is None or (group[0][1] + group[1][1]) % SUB:
            group = units[at : at + 1]
        at += len(group)
        first = group[0][0]
        size = sum(g[1] for g in group)
        blocks_in = []
        for partner, carry in sources:
            value = partner[:, first : first + size].astype(F32)
            start_part = value[:SPAN] + carry[:, first : first + size]
            blocks_in.append(jnp.concatenate([start_part, value[SPAN:]], axis=0))
        for f, width, here, ones in group:
            parts = ([], [])
            for n in range(0, len(sources), 2):
                a = blocks_in[n][:, f - first : f - first + width].reshape(STEPS * width, LANES)
                b = blocks_in[n + 1][:, f - first : f - first + width]
                b = b.reshape(STEPS * width, LANES)
                low = lax.broadcasted_iota(jnp.int32, a.shape, 1) < R
                parts[0].append(jnp.where(low, a, pltpu.roll(b, R, 1)).astype(BF16))
                parts[1].append(jnp.where(low, pltpu.roll(a, R, 1), b).astype(BF16))
            total = 0.0
            for r in (0, 1):
                total = total + dot_tn(ones[r], jnp.concatenate(parts[r], axis=1))
            target[here, :] = target[here, :] + total


def row_masks(owned, start, blocks, atoms):
    for n, (at, width, size) in enumerate(blocks):
        _, molecule, _ = row_parts((width, LANES), 0, size)
        first = start - HALO + (n * BLOCK + molecule) * MOL
        owned[at : at + width] = jnp.where((first >= 0) & (first < atoms), 1.0, 0.0)


def set_multiplicities(count, target, blocks, rows):
    lane = lax.broadcasted_iota(jnp.int32, (rows, LANES), 1)
    inner = jnp.where(lane >= R, lane - R, lane)
    last = []
    for _, width, size in blocks:
        last.append(row_parts((width, LANES), 0, size)[0])
    doubled = (jnp.concatenate(last, axis=0) == ROW_GROUPS - 1) & (lane >= R)
    for t in range(SPAN):
        value = jnp.where(inner < 32, count[t], 0.0)
        for k in range(1, OFFSETS + 1):
            value = jnp.where(inner == 32 + k, count[t + k], value)
        if t == SPAN - 1:
            value = jnp.where(doubled, 0.0, value)
        target[t] = value


def dot(a, b):
    return jnp.dot(a, b, preferred_element_type=F32)


def dot_tn(a, b):
    return lax.dot_general(a, b, (((0,), (0,)), ((), ())), preferred_element_type=F32)


def dot_nt(a, b):
    return lax.dot_general(a, b, (((1,), (1,)), ((), ())), preferred_element_type=F32)


COSINE = (0.9999999998, -0.04934802137, 0.000405870916, -1.335212003e-06, 2.349373138e-09, -2.43963243e-12)

GEO_ENVELOPE, GEO_BEND, GEO_INVERSE, GEO_INTO, GEO_FROM, GEO_WAY, GEO_SLOPE, GEO_OWN = 0, 1, 2, 3, 4, 5, 8, 9
GEO = 10


def geometry(pos, many, t, rows, owned, radial, geo):
    inv_space = (R - 1) / CUTOFF

    def step(k, _):
        for o, size in halves(rows):
            here = pl.ds(pl.multiple_of(k * rows + o, SUB), size)
            part = slice(o, o + size)
            off = [p[t, part] - p[t + 1 + k, part] for p in pos]
            mine = owned[part].astype(BF16)
            close = many[t, part]
            lane = lax.broadcasted_iota(jnp.int32, (size, LANES), 1)
            base = jnp.where(lane >= R, R, 0)
            centre = (lane - base).astype(F32)
            near = base + (k + 1)
            square = off[0] * off[0] + off[1] * off[1] + off[2] * off[2]
            clamped = jnp.maximum(square, 0.01)
            inverse = lax.rsqrt(clamped)
            c = COSINE[-1]
            for term in COSINE[-2::-1]:
                c = c * clamped + term
            c = jnp.where(clamped < CUTOFF * CUTOFF, c, 0.0)
            envelope = c * c
            y = jnp.maximum(1.0 - envelope, 1e-30)
            bend = ((-math.pi / CUTOFF) * c) * (y * lax.rsqrt(y))
            u = (clamped * inverse) * inv_space - centre
            bump = jnp.exp(-0.5 * (u * u))
            value = bump * envelope
            high = value.astype(BF16)
            slope = bump * bend - inv_space * (u * value)
            radial[here, :LANES] = high
            radial[here, LANES:] = (value - high.astype(F32)).astype(BF16)
            geo[GEO_OWN, here, :] = high * mine
            geo[GEO_SLOPE, here, :] = slope.astype(BF16)
            geo[GEO_BEND, here, :] = bend.astype(BF16)
            geo[GEO_ENVELOPE, here, :] = envelope.astype(BF16)
            for d in range(3):
                geo[GEO_WAY + d, here, :] = (off[d] * inverse).astype(BF16)
            signed = jnp.where(square > 0.01, inverse, -inverse)
            geo[GEO_INVERSE, here, :] = signed.astype(BF16)
            into = jnp.take_along_axis(close, near, axis=1)
            out_of = jnp.take_along_axis(close, near + 32, axis=1)
            geo[GEO_INTO, here, :] = into.astype(BF16)
            geo[GEO_FROM, here, :] = out_of.astype(BF16)
        return 0

    lax.fori_loop(0, OFFSETS, step, 0)


def halves(rows):
    tiles = rows // SUB
    first = (tiles + 1) // 2 * SUB
    return ((0, first), (first, rows - first))


def set_filters(weights_ref, filter_1, filter_2):
    weights_ref[...] = jnp.zeros(weights_ref.shape, BF16)
    for f, ref in enumerate((filter_1, filter_2)):
        half = ref[...] * jnp.asarray(0.5, BF16)
        for part in range(2):
            for g in range(LANE_GROUPS):
                down = part * LANES + g * R
                at = f * LANES + g * R
                weights_ref[down : down + R, at : at + R] = half


def gate(h):
    t = jnp.tanh(h)
    u = 1.0 + t
    f = h * u
    return f.astype(BF16), (u + f * (1.0 - t)).astype(BF16)


def carried(rows, t, totals, group, body):
    def outer(s, _):
        o = pl.multiple_of(s * SUB, SUB)
        block = pl.ds(o, SUB)
        ii = (t, block)
        sums = None
        for k in range(0, OFFSETS, group):
            loaded = []
            for n in range(k, k + group):
                here = pl.ds(o + n * rows, SUB)
                loaded.append(body(o, here, ii, (t + 1 + n, block), n))
            done = [f() for f in loaded]
            given = [one for one, _ in done]
            while len(given) > 1:
                left = given[len(given) // 2 * 2 :]
                pairs = zip(given[0::2], given[1::2])
                given = [[x + y for x, y in zip(a, b)] for a, b in pairs] + left
            total = [x.astype(F32) for x in given[0]]
            sums = total if sums is None else [x + y for x, y in zip(sums, total)]
            for _, stores in done:
                for ref, index, value in stores:
                    ref[index] = value
        for total, value in zip(totals, sums):
            total[ii] = value
        return 0

    lax.fori_loop(0, rows // SUB, outer, 0)


def geometry_kernel(
    molecules, rows, atoms,
    scalars, rows_ref, radial_out, geo_out, owned, near, near_last, px, py, pz, many, stage,
):
    t = pl.program_id(0)
    start = scalars[0]
    blocks = block_list(molecules, rows)
    distances = (near, near_last)

    @pl.when(t == 0)
    def _():
        row_masks(owned, start, blocks, atoms)
        set_distances(near, blocks[0][1], blocks[0][2])
        set_distances(near_last, blocks[-1][1], blocks[-1][2])
        lanes = slice(POS * LANES, (POS + 1) * LANES)
        spread_positions(rows_ref, lanes, (px, py, pz), blocks, distances, start)
        lanes = slice(C2_COUNT * LANES, (C2_COUNT + 1) * LANES)
        spread(rows_ref, lanes, stage, blocks, distances, start)
        set_multiplicities(stage.at[1], many, blocks, rows)

    geometry((px, py, pz), many, t, rows, owned, radial_out.at[0], geo_out.at[0])


def vector_kernel(
    molecules, rows, atoms,
    scalars, rows_ref, filter_1, filter_2, radial_in, geo_in, pull_in,
    sums_ref, back_ref, grads_ref, pos_out, grad_w_ref,
    weights_ref, near, near_last, stage, loose, pre, grad_pre,
    grad_radial, grad_ways,
    w0, w1, w2, v2, c0, c1, c2,
    s0, s1, s2, a0, a1, a2, gv, gx, gy, gz,
    fs0, fs1, fs2, fa0, fa1, fa2, fgv, fgx, fgy, fgz,
):
    t = pl.program_id(0)
    start = scalars[0]
    own = slice(HALO, HALO + atoms)
    radial, geo = radial_in.at[0], geo_in.at[0]
    w, c, g_pos = (w0, w1, w2), (c0, c1, c2), (gx, gy, gz)
    sums, backs = (s0, s1, s2), (a0, a1, a2)
    blocks = block_list(molecules, rows)
    distances = (near, near_last)

    @pl.when(t == 0)
    def _():
        set_filters(weights_ref, filter_1, filter_2)
        set_distances(near, blocks[0][1], blocks[0][2])
        set_distances(near_last, blocks[-1][1], blocks[-1][2])
        lanes = slice(W01 * LANES, (C2_COUNT + 1) * LANES)
        spread(rows_ref, lanes, stage, blocks, distances, start)
        for n, target in enumerate((w0, w1, w2, v2, c0, c1, c2)):
            target[...] = stage[n].astype(BF16)
        for total in (s0, s1, s2, a0, a1, a2, gv, gx, gy, gz):
            total[...] = jnp.zeros(total.shape, BF16)
        grad_w_ref[...] = jnp.zeros(grad_w_ref.shape, F32)

    pre[...] = dot(radial[...], weights_ref[...])

    def channel(o, here, ii, jj, k):
        h1, h2 = pre[here, :LANES], pre[here, LANES:]
        ni, nj = geo[GEO_INTO, here, :], geo[GEO_FROM, here, :]
        v2i, v2j = v2[ii], v2[jj]
        ways = [geo[GEO_WAY + d, here, :] for d in range(3)]
        wi, wj = [w[d][ii] for d in range(3)], [w[d][jj] for d in range(3)]
        ci, cj = [c[d][ii] for d in range(3)], [c[d][jj] for d in range(3)]
        old_sums = [sums[d][jj] for d in range(3)]
        old_backs = [backs[d][jj] for d in range(3)]
        old_gv = gv[jj]

        def compute():
            f1, d1 = gate(h1)
            f2, d2 = gate(h2)
            f1i, f1j, f2i, f2j = f1 * ni, f1 * nj, f2 * ni, f2 * nj
            msg_i, msg_j = f2i * v2j, f2j * v2i
            stores, sum_i, back_i = [], [], []
            along_i = along_j = across_i = across_j = None
            for d in range(3):
                way = ways[d]
                sum_i.append(f1i * wj[d] + msg_i * way)
                stores.append((sums[d], jj, old_sums[d] + (f1j * wi[d] - msg_j * way)))
                stores.append((backs[d], jj, old_backs[d] + f1i * ci[d]))
                back_i.append(f1j * cj[d])
                grad = ci[d] * msg_i - cj[d] * msg_j
                stores.append((grad_ways, (d, here, slice(None)), grad))
                new = (ci[d] * way, cj[d] * way, ci[d] * wj[d], cj[d] * wi[d])
                if d == 0:
                    along_i, along_j, across_i, across_j = new
                else:
                    along_i, along_j = along_i + new[0], along_j + new[1]
                    across_i, across_j = across_i + new[2], across_j + new[3]
            stores.append((gv, jj, old_gv + f2i * along_i))
            g1 = ni * across_i + nj * across_j
            g2 = ni * along_i * v2j - nj * along_j * v2i
            stores.append((grad_pre, (here, slice(0, LANES)), g1 * d1))
            stores.append((grad_pre, (here, slice(LANES, None)), g2 * d2))
            return sum_i + back_i + [-(f2j * along_j)], stores

        return compute

    carried(rows, t, (fs0, fs1, fs2, fa0, fa1, fa2, fgv), 2, channel)
    grad_radial[...] = dot_nt(grad_pre[...], weights_ref[:LANES])
    grad_w_ref[...] = grad_w_ref[...] + dot_tn(geo[GEO_OWN], grad_pre[...])

    def turn(o, here, ii, jj, k):
        ways = [geo[GEO_WAY + d, here, :] for d in range(3)]
        grads = [grad_ways[d, here, :] for d in range(3)]
        grad, slope = grad_radial[here, :], geo[GEO_SLOPE, here, :]
        signed, more = geo[GEO_INVERSE, here, :], pull_in[0, here, :]
        old = [g[jj] for g in g_pos]

        def compute():
            inverse = jnp.abs(signed)
            turned = [g * inverse for g in grads]
            along = ways[0] * turned[0] + ways[1] * turned[1] + ways[2] * turned[2]
            pull = jnp.where(signed > 0, grad.astype(BF16) * slope + more - along, 0)
            out = [turned[d] + ways[d] * pull for d in range(3)]
            return out, [(g_pos[d], jj, old[d] - out[d]) for d in range(3)]

        return compute

    carried(rows, t, (fgx, fgy, fgz), 7, turn)

    @pl.when(t == SPAN - 1)
    def _():
        low = lax.broadcasted_iota(jnp.int32, (atoms, LANES), 1) < R
        totals = (s0, s1, s2, gv, a0, a1, a2, gx, gy, gz)
        firsts = (fs0, fs1, fs2, fgv, fa0, fa1, fa2, fgx, fgy, fgz)
        collect(tuple(zip(totals, firsts)), loose, blocks, distances, start)
        both = loose[own, :LANES].T
        sums_ref[0] = both[:R]
        sums_ref[1] = both[R:]
        both = loose[own, LANES : 2 * LANES].T
        sums_ref[2] = both[:R]
        grads_ref[R:] = both[R:].astype(BF16)

        def kept(n):
            return rows_ref[own, n * LANES : (n + 1) * LANES].astype(F32)

        v12 = kept(V12)
        v11 = jnp.where(low, v12, pltpu.roll(v12, R, 1))
        back = loose[own, 2 * LANES : 3 * LANES]
        both = (back * v11).T
        back_ref[0] = both[:R]
        back_ref[1] = both[R:]
        partial = back * kept(VEC01)
        partial = partial + pltpu.roll(partial, R, 1)
        back = loose[own, 3 * LANES : 4 * LANES]
        back_ref[2] = (back * v11).T[:R]
        partial = partial + back * kept(VEC2)
        grads_ref[:R] = partial.T[:R].astype(BF16)
        pos_out[...] = jnp.zeros(pos_out.shape, F32)
        pos_out[0:1] = jnp.sum(back.T[R:], axis=0, keepdims=True)
        both = loose[own, 4 * LANES :].T
        pos_out[1:2] = jnp.sum(both[:R], axis=0, keepdims=True)
        pos_out[2:3] = jnp.sum(both[R:], axis=0, keepdims=True)


def scalar_kernel(
    molecules, rows, atoms,
    scalars, rows_ref, filter_1, filter_2, scalar_parts, radial_in, geo_in,
    sum_ref, grads_ref, grad_w_ref, pull_out,
    weights_ref, heads_ref, near, near_last, stage, loose, loose_low, pre,
    grad_pre, grad_radial, products, sums, gates, bends,
    q, key, v0, gs,
    ss, gq, gk, g0,
    fss, fgq, fgk, fg0,
):
    t = pl.program_id(0)
    start = scalars[0]
    own = slice(HALO, HALO + atoms)
    radial, geo = radial_in.at[0], geo_in.at[0]
    blocks = block_list(molecules, rows)
    distances = (near, near_last)

    @pl.when(t == 0)
    def _():
        set_filters(weights_ref, filter_1, filter_2)
        row = lax.broadcasted_iota(jnp.int32, (2 * LANES, 2 * LANES), 0)
        lane = lax.broadcasted_iota(jnp.int32, (2 * LANES, 2 * LANES), 1)
        heads_ref[...] = jnp.where(row // HEAD == lane // HEAD, 1.0, 0.0).astype(BF16)
        set_distances(near, blocks[0][1], blocks[0][2])
        set_distances(near_last, blocks[-1][1], blocks[-1][2])
        lanes = slice(QK * LANES, (V0_COUNT + 1) * LANES)
        spread(rows_ref, lanes, stage, blocks, distances, start)
        for n, target in enumerate((q, key, v0)):
            target[...] = stage[n].astype(BF16)
        summed = scalar_parts[0].astype(F32)
        for f in range(1, scalar_parts.shape[0]):
            summed = summed + scalar_parts[f].astype(F32)
        summed = jnp.concatenate([summed, jnp.zeros_like(summed)], axis=0).T.astype(BF16)
        loose_low[own] = summed[:atoms]
        loose_low[:HALO] = summed[atoms : atoms + HALO]
        loose_low[HALO + atoms : 2 * HALO + atoms] = summed[atoms + HALO : atoms + 2 * HALO]
        end = 2 * HALO + atoms
        loose_low[end:] = jnp.zeros((loose_low.shape[0] - end, LANES), BF16)
        spread(loose_low, slice(None), stage, blocks, distances, start)
        gs[...] = stage[0].astype(BF16)
        for total in (ss, gq, gk, g0):
            total[...] = jnp.zeros(total.shape, BF16)
        grad_w_ref[...] = jnp.zeros(grad_w_ref.shape, F32)

    pre[...] = dot(radial[...], weights_ref[...])

    def multiply(k, _):
        for o, size in halves(rows):
            here = pl.ds(pl.multiple_of(k * rows + o, SUB), size)
            ii, jj = (t, slice(o, o + size)), (t + 1 + k, slice(o, o + size))
            fk, dk = gate(pre[here, :LANES])
            f0, d0 = gate(pre[here, LANES:])
            k_ij, k_ji = q[ii] * key[jj] * fk, q[jj] * key[ii] * fk
            s_ij, s_ji = gs[ii] * v0[jj] * f0, gs[jj] * v0[ii] * f0
            gates[0, here, :] = fk
            gates[1, here, :] = f0
            gates[2, here, :] = dk
            gates[3, here, :] = d0
            products[0, here, :LANES] = k_ij
            products[0, here, LANES:] = k_ji
            products[1, here, :LANES] = s_ij
            products[1, here, LANES:] = s_ji
        return 0

    lax.fori_loop(0, OFFSETS, multiply, 0)
    sums[0] = dot(products[0], heads_ref[...])
    sums[1] = dot(products[1], heads_ref[...])

    def channel(o, here, ii, jj, k):
        fk, f0, dk, d0 = [gates[n, here, :] for n in range(4)]
        envelope, bend = geo[GEO_ENVELOPE, here, :], geo[GEO_BEND, here, :]
        side_in = []
        for side in range(2):
            lanes = slice(side * LANES, (side + 1) * LANES)
            m = geo[GEO_INTO + side, here, :]
            h, o_ = (ii, jj) if side == 0 else (jj, ii)
            side_in.append(
                (m, sums[0, here, lanes], sums[1, here, lanes])
                + (q[h], key[o_], gs[h], v0[o_])
            )
        old = [ref[jj] for ref in (g0, gk, ss, gq)]

        def compute():
            gives, news = [], []
            for m, score, g_att, qh, kt, gh, vt in side_in:
                act, rise = gate(0.5 * score)
                g_att = g_att.astype(BF16)
                weight = m * envelope
                att = act * weight
                g_score = g_att * (0.5 * rise) * weight
                lift = m * (g_att * act)
                bv, dv = f0 * att, fk * g_score
                gives.append((vt * bv, kt * dv, gh * bv, qh * dv))
                news.append((qh * kt * g_score, gh * vt * att, lift))
            one, two = gives
            new = [x + y for x, y in zip(*news)]
            stores = [
                (ref, jj, x + y)
                for ref, x, y in zip((g0, gk, ss, gq), old, (one[2], one[3], two[0], two[1]))
            ]
            stores.append((grad_pre, (here, slice(0, LANES)), new[0] * dk))
            stores.append((grad_pre, (here, slice(LANES, None)), new[1] * d0))
            stores.append((bends, (here, slice(None)), new[2] * bend * (1.0 / HEAD)))
            return [one[0], one[1], two[2], two[3]], stores

        return compute

    carried(rows, t, (fss, fgq, fg0, fgk), 2, channel)
    grad_radial[...] = dot_nt(grad_pre[...], weights_ref[:LANES])
    grad_w_ref[...] = grad_w_ref[...] + dot_tn(geo[GEO_OWN], grad_pre[...])

    def pull(k, _):
        here = pl.ds(pl.multiple_of(k * rows, SUB), rows)
        grad = grad_radial[here, :].astype(BF16)
        pull_out[0, here, :] = grad * geo[GEO_SLOPE, here, :] + bends[here, :]
        return 0

    lax.fori_loop(0, OFFSETS, pull, 0)

    @pl.when(t == SPAN - 1)
    def _():
        totals = (ss, g0, gq, gk)
        firsts = (fss, fg0, fgq, fgk)
        collect(tuple(zip(totals, firsts)), loose, blocks, distances, start)
        both = loose[own, :LANES].T
        sum_ref[...] = both[:R].astype(BF16)
        grads_ref[2 * R :] = both[R:].astype(BF16)
        grads_ref[: 2 * R] = loose[own, LANES : 2 * LANES].T.astype(BF16)


def whole(memory=pltpu.VMEM):
    return pl.BlockSpec(memory_space=memory)


def params(mib=60):
    return pltpu.CompilerParams(vmem_limit_bytes=mib * 1024 * 1024)


def edge_sizes(atoms):
    molecules = (atoms + 2 * (MOL - 1)) // MOL
    full, rest = divmod(molecules, BLOCK)
    rows = full * ROW_GROUPS * BLOCK + -(-ROW_GROUPS * rest // BLOCK) * BLOCK
    rows = -(-rows // SUB) * SUB
    tall = -(-(HALO + molecules * MOL) // SUB) * SUB
    return molecules, rows, tall


def by_step(shape):
    zeros = (0,) * (len(shape) - 1)
    return pl.BlockSpec((1,) + shape[1:], lambda t: (t,) + zeros)


def fixed(shape):
    zeros = (0,) * len(shape)
    return pl.BlockSpec(shape, lambda t: zeros)


def edge_call(kernel, atoms, inputs, stepped_in, outs, stepped_out, scratch):
    molecules, rows, _ = edge_sizes(atoms)
    return pl.pallas_call(
        functools.partial(kernel, molecules, rows, atoms),
        grid=(SPAN,),
        out_shape=[jax.ShapeDtypeStruct(s, kind) for s, kind in outs + stepped_out],
        in_specs=[whole(pltpu.SMEM)]
        + [fixed(x.shape) for x in inputs[1:]]
        + [by_step(x.shape) for x in stepped_in],
        out_specs=[fixed(s) for s, _ in outs] + [by_step(s) for s, _ in stepped_out],
        scratch_shapes=[pltpu.VMEM(s, kind) for s, kind in scratch],
        compiler_params=params(),
        cost_estimate=pl.CostEstimate(
            flops=20 * 10**9, bytes_accessed=40 * 10**6, transcendentals=10**7
        ),
    )(*inputs, *stepped_in)


def shared_scratch(atoms):
    molecules, rows, tall = edge_sizes(atoms)
    batch = OFFSETS * rows
    blocks = block_list(molecules, rows)
    return {
        "weights": ((2 * LANES, 2 * LANES), BF16),
        "many": ((SPAN, rows, LANES), F32),
        "stage2": ((2, STEPS, rows, LANES), F32),
        "mask": ((rows, LANES), F32),
        "near": ((LANE_GROUPS, STEPS * blocks[0][1], WINDOW), jnp.int32),
        "near_last": ((LANE_GROUPS, STEPS * blocks[-1][1], WINDOW), jnp.int32),
        "stage8": ((8, STEPS, rows, LANES), F32),
        "stage4": ((4, STEPS, rows, LANES), F32),
        "loose5": ((tall, 5 * LANES), F32),
        "loose2": ((tall, 2 * LANES), F32),
        "loose_low": ((tall, LANES), BF16),
        "tall": ((STEPS, rows, LANES), F32),
        "low": ((STEPS, rows, LANES), BF16),
        "first": ((SPAN, rows, LANES), F32),
        "pre": ((batch, 2 * LANES), F32),
        "grad_pre": ((batch, 2 * LANES), BF16),
        "line": ((batch, LANES), F32),
        "line2": ((2, batch, LANES), BF16),
        "line3": ((3, batch, LANES), BF16),
        "line4": ((4, batch, LANES), BF16),
        "line1": ((batch, LANES), BF16),
        "wide2": ((2, batch, 2 * LANES), BF16),
        "wide2f": ((2, batch, 2 * LANES), F32),
    }


def offsets_in_block(neighbours, mask, first):
    lane = lax.broadcasted_iota(jnp.int32, neighbours.shape, 1)
    diff = neighbours - (first + lane)
    return jnp.where(diff < 0, diff + MOL, diff) * mask


def pieces(x):
    a = x.astype(BF16)
    rest = x - a.astype(F32)
    b = rest.astype(BF16)
    return a, b, (rest - b.astype(F32)).astype(BF16)


def edge_groups(features, vectors, cot_f, cot_v, neighbours, mask, positions, first):
    diff = offsets_in_block(neighbours[...], mask[...], first).astype(F32).astype(BF16)
    groups = [jnp.concatenate([features[...], cot_f[...], diff], axis=0)]
    for d in range(3):
        rows = [x.astype(F32) for x in pieces(positions[d : d + 1])]
        rows = jnp.concatenate(rows + [jnp.zeros((29, LANES), F32)], axis=0).astype(BF16)
        groups.append(jnp.concatenate([vectors[d], cot_v[d], rows], axis=0))
    return groups


def halo_kernel(atoms, scalars, *refs):
    row_first = scalars[2]
    lane = lax.broadcasted_iota(jnp.int32, (GROUP_ROWS, LANES), 1)
    for end, at, out in ((0, atoms - LANES, refs[14]), (1, 0, refs[15])):
        groups = edge_groups(*refs[7 * end : 7 * end + 7], row_first + at)
        total = None
        for g, group in enumerate(groups):
            by = (HALO * (g + 1) if end == 0 else HALO * g) % LANES
            moved = group.astype(F32)
            moved = pltpu.roll(moved, by, 1) if by else moved
            total = moved if total is None else jnp.where(lane >= HALO * g, moved, total)
        out[...] = total.astype(BF16)


def halo_call(atoms, scalars, arrays):
    specs = []
    for at in (atoms // LANES - 1, 0):
        for x in arrays:
            shape = x.shape[:-1] + (LANES,)
            index = (0,) * (x.ndim - 1) + (at,)
            specs.append(pl.BlockSpec(shape, lambda *_, index=index: index))
    out = jax.ShapeDtypeStruct((GROUP_ROWS, LANES), BF16)
    return pl.pallas_call(
        functools.partial(halo_kernel, atoms),
        grid=(1,),
        out_shape=[out, out],
        in_specs=[whole(pltpu.SMEM)] + specs,
        out_specs=[whole(), whole()],
        compiler_params=params(),
    )(scalars, *arrays, *arrays)


def column(row):
    return jnp.broadcast_to(row, (8, row.shape[1])).T[:, :1]


def normalised(f):
    mean = jnp.mean(f, axis=0, keepdims=True)
    centred = f - mean
    inv = lax.rsqrt(jnp.mean(centred * centred, axis=0, keepdims=True) + EPSILON)
    return centred * inv, mean, inv


def dense_kernel(
    atoms,
    scalars, features, vectors, cot_f, cot_v, neighbours, mask, positions, low_ref, high_ref,
    gain_ref, bias_ref, w_query, w_key, w_value, w_vector, w_output,
    rows_ref, part_ref, stat_ref,
    w_qk, w_v0, w_v12, w_vec_t, w_out,
):
    chan_first = pl.multiple_of(scalars[1], R)
    row_first = scalars[2]
    gain, bias = column(gain_ref[...]), column(bias_ref[...])
    w_qk[:R] = w_query[...]
    w_qk[R:] = w_key[...]
    w_v0[:R] = w_value[0]
    w_v0[R:] = jnp.zeros((R, H), BF16)
    w_v12[:R] = w_value[1]
    w_v12[R:] = w_value[2]
    for p in range(3):
        w_vec_t[p * R : (p + 1) * R] = w_vector[p]
    w_out[...] = jnp.concatenate([w_output[p] for p in range(3)], axis=0).astype(F32).T.astype(BF16)

    def block(f, v, cf, cv, own_v, diff, pos):
        width = f.shape[1]
        normed, mean, inv = normalised(f)
        turned = (normed * gain + bias).T.astype(BF16)
        kinds = lax.broadcasted_iota(jnp.int32, (R, width), 0)
        kinds = jnp.where(kinds < 32, kinds, MOL + 32 - kinds).astype(F32)
        counts = jnp.zeros((R, width), F32)
        for s in range(diff.shape[0]):
            counts = counts + jnp.where(diff[s : s + 1] == kinds, 1.0, 0.0)
        none = jnp.zeros((R, width), F32)
        counts = jnp.concatenate([none, counts], axis=0).T
        low = lax.broadcasted_iota(jnp.int32, (width, LANES), 1) < R
        pairs = [None] * 10
        pairs[QK] = dot_nt(turned, w_qk[...])
        pairs[V0_COUNT] = dot_nt(turned, w_v0[...]) + counts
        v12 = dot_nt(turned, w_v12[...]).astype(BF16).astype(F32)
        v11 = jnp.where(low, v12, pltpu.roll(v12, R, 1))
        pairs[V12] = v12
        pairs[VEC01] = jnp.concatenate([own_v[0], own_v[1]], axis=0).T
        pairs[VEC2] = jnp.concatenate([own_v[2], none], axis=0).T
        pairs[W01] = pairs[VEC01] * v11
        pairs[W2V2] = jnp.where(low, pairs[VEC2] * v11, v12)
        pairs[C01] = jnp.concatenate([cv[0], cv[1]], axis=0).T
        pairs[C2_COUNT] = jnp.concatenate([cv[2], none], axis=0).T + counts
        pairs[POS] = jnp.concatenate([pos, jnp.zeros((LANES - 9, width), F32)], axis=0).T
        vec_dot = grad_0 = 0.0
        for d in range(3):
            proj = dot(w_vec_t[...], v[d])
            vec_dot = vec_dot + proj[:R] * proj[R : 2 * R]
            grad_0 = grad_0 + cv[d] * proj[2 * R :]
        grad_out = jnp.concatenate([grad_0, cf * vec_dot, cf], axis=0).astype(BF16)
        part = dot(w_out[...], grad_out)
        return [x.astype(BF16) for x in pairs], part.astype(BF16), mean, inv

    wide = 2 * LANES

    def step(b, _):
        at = pl.multiple_of(b * wide, wide)
        here = pl.ds(at, wide)
        own_v = [vectors[d, pl.ds(chan_first, R), here].astype(F32) for d in range(3)]
        diff = offsets_in_block(neighbours[:, here], mask[:, here], row_first + at)
        places = [p.astype(F32) for d in range(3) for p in pieces(positions[d : d + 1, here])]
        pairs, part, mean, inv = block(
            features[:, here].astype(F32),
            [vectors[d, :, here] for d in range(3)],
            cot_f[:, here].astype(F32),
            [cot_v[d, :, here].astype(F32) for d in range(3)],
            own_v,
            diff.astype(F32),
            jnp.concatenate(places, axis=0),
        )
        there = pl.ds(pl.multiple_of(HALO + at, 2 * SUB), wide)
        for n, pair in enumerate(pairs):
            rows_ref[there, n * LANES : (n + 1) * LANES] = pair
        part_ref[:, here] = part
        stat_ref[0:1, here] = mean
        stat_ref[1:2, here] = inv
        return 0

    lax.fori_loop(0, atoms // wide, step, 0)

    lane = lax.broadcasted_iota(jnp.int32, (GROUP_ROWS, LANES), 1)
    packed_low, packed_high = low_ref[...].astype(F32), high_ref[...].astype(F32)
    groups = []
    for g in range(4):
        a = pltpu.roll(packed_low, (LANES - HALO * g) % LANES, 1) if g else packed_low
        by = (LANES + HALO - HALO * g) % LANES
        b = pltpu.roll(packed_high, by, 1) if by else packed_high
        both = jnp.where(lane < HALO, a, jnp.where(lane < 2 * HALO, b, 0.0))
        groups.append(both)
    pick_rows = lax.broadcasted_iota(jnp.int32, (H, LANES), 0)
    own_v, pos = [], []
    for d in range(3):
        g = groups[1 + d]
        found = g[:R]
        for f in range(1, H // R):
            found = jnp.where(chan_first == f * R, g[f * R : (f + 1) * R], found)
        own_v.append(found)
        pos.append(g[320:323])
    pairs, part, _, _ = block(
        groups[0][:H],
        [groups[1 + d][:H].astype(BF16) for d in range(3)],
        groups[0][H : H + R],
        [groups[1 + d][H : H + R] for d in range(3)],
        own_v,
        groups[0][H + R :],
        jnp.concatenate(pos, axis=0),
    )
    high = HALO + atoms
    tall = rows_ref.shape[0]
    for n, pair in enumerate(pairs):
        lanes = slice(n * LANES, (n + 1) * LANES)
        rows_ref[:HALO, lanes] = pair[:HALO]
        rows_ref[high : high + HALO, lanes] = pair[HALO : 2 * HALO]
        rows_ref[high + HALO :, lanes] = jnp.zeros((tall - high - HALO, LANES), BF16)
    part_ref[:, atoms:] = part


def both_diagonals(grad, f):
    at = f * LANES
    return 0.5 * (grad[:R, at : at + R] + grad[R:, at + R : at + LANES])


def filter_block(grad):
    both = jnp.concatenate([both_diagonals(grad, 0), both_diagonals(grad, 1)], axis=1)
    return jnp.concatenate([both[: R // 2], both[R // 2 :]], axis=1)


def layer_kernel(
    atoms,
    scalars, features, stat, vectors, cot_f, cot_v, gathered, grads_b, gain_ref, bias_ref,
    w_vector, w_output, grad_filters_b,
    feat_out, delta_ref, square_ref, send_ref, flat_ref,
    w_vec, w_vec_t, w_out_t,
):
    chan_first = pl.multiple_of(scalars[1], R)
    gain, bias = column(gain_ref[...]), column(bias_ref[...])
    for p in range(3):
        w_vec_t[p * R : (p + 1) * R] = w_vector[p]
        w_out_t[p * R : (p + 1) * R] = w_output[p]
    w_vec[...] = w_vec_t[...].astype(F32).T.astype(BF16)
    t_vec, t_out, t_b = [flat_ref.at[n * 3 * R : (n + 1) * 3 * R] for n in range(3)]
    flat_ref[...] = jnp.zeros(flat_ref.shape, F32)
    wide = 2 * LANES
    split = send_ref.shape[0]

    def step(b, _):
        at = pl.multiple_of(b * wide, wide)
        here = pl.ds(at, wide)
        all_sums = gathered[:, here]
        outputs = dot(w_out_t[...], all_sums)
        out_0, out_1, out_2 = outputs[:R], outputs[R : 2 * R], outputs[2 * R :]
        cf = cot_f[:, here].astype(F32)
        grad_dot = cf * out_1
        vec_dot = grad_0 = 0.0
        for d in range(3):
            proj = dot(w_vec_t[...], vectors[d, :, here])
            first, second, third = proj[:R], proj[R : 2 * R], proj[2 * R :]
            cv = cot_v[d, :, here].astype(F32)
            vec_dot = vec_dot + first * second
            grad_0 = grad_0 + cv * third
            delta_ref[d, :, here] = third * out_0
            grad_proj = jnp.concatenate(
                [grad_dot * second, grad_dot * first, cv * out_0], axis=0
            ).astype(BF16)
            part = dot(w_vec[...], grad_proj).astype(BF16)
            for f in range(split):
                send_ref[f, d * R : (d + 1) * R, here] = part[f * R : (f + 1) * R]
            t_vec[...] = t_vec[...] + dot_nt(grad_proj, vectors[d, :, here])
        delta = vec_dot * out_1 + out_2
        moved = features[pl.ds(chan_first, R), here].astype(F32) + delta
        feat_out[:, here] = moved.astype(BF16)
        grad_out = jnp.concatenate([grad_0, cf * vec_dot, cf], axis=0).astype(BF16)
        t_out[...] = t_out[...] + dot_nt(grad_out, all_sums)
        square_ref[0:1, here] = jnp.sum(moved * moved, axis=0, keepdims=True)
        square_ref[1:2, here] = jnp.sum(delta * delta, axis=0, keepdims=True)
        normed = (features[:, here].astype(F32) - stat[0:1, here]) * stat[1:2, here]
        normal = (normed * gain + bias).astype(BF16)
        t_b[...] = t_b[...] + dot_nt(grads_b[:, here], normal)
        return 0

    lax.fori_loop(0, atoms // wide, step, 0)
    flat_ref[9 * R :] = filter_block(grad_filters_b[...])


def normal_kernel(
    atoms,
    scalars, features, stat, vectors, delta_ref, square_ref, sums_ref,
    grads_b, grads_a, pos_a, mask, gain_ref, bias_ref,
    w_query, w_key, w_value, grad_filters_a,
    vec_out, send_ref, flat_ref,
    w_five, t_late,
):
    chan_first = pl.multiple_of(scalars[1], R)
    gain, bias = column(gain_ref[...]), column(bias_ref[...])
    five = [w_query[...], w_key[...]] + [w_value[p] for p in range(3)]
    w_five[...] = jnp.concatenate(five, axis=0).astype(F32).T.astype(BF16)
    t_late[...] = jnp.zeros(t_late.shape, F32)
    wide = 2 * LANES
    split = send_ref.shape[0]

    def step(b, _):
        at = pl.multiple_of(b * wide, wide)
        here = pl.ds(at, wide)
        real = mask[:, here].astype(F32)
        square_v = square_dv = 0.0
        for d in range(3):
            delta = delta_ref[d, :, here] + sums_ref[d, :, here]
            moved = vectors[d, pl.ds(chan_first, R), here].astype(F32) + delta
            vec_out[d, :, here] = moved.astype(BF16)
            square_v = square_v + moved * moved
            square_dv = square_dv + delta * delta
        normed = (features[:, here].astype(F32) - stat[0:1, here]) * stat[1:2, here]
        normal = (normed * gain + bias).astype(BF16)
        grads = jnp.concatenate([grads_b[:, here], grads_a[:, here]], axis=0)
        t_late[...] = t_late[...] + dot_nt(grads_a[:, here], normal)
        part = dot(w_five[...], grads)
        rounded = part.astype(BF16)
        for f in range(split):
            send_ref[f, :R, here] = rounded[f * R : (f + 1) * R]
        hat = part * gain
        tops = [
            jnp.sum(hat, axis=0, keepdims=True),
            jnp.sum(hat * normed, axis=0, keepdims=True),
        ]
        exact = [pos_a[d : d + 1, here] for d in range(3)]
        exact += [square_ref[n : n + 1, here] * real for n in range(2)]
        for x in (square_v, square_dv):
            exact.append(jnp.sum(x, axis=0, keepdims=True) * real)
        heads = [x.astype(BF16).astype(F32) for x in exact]
        tops = tops + heads + [x - y for x, y in zip(exact, heads)]
        tops = jnp.concatenate(tops, axis=0).astype(BF16)
        for f in range(split):
            send_ref[f, R:, here] = tops
        return 0

    lax.fori_loop(0, atoms // wide, step, 0)
    flat_ref[: 2 * R] = t_late[...].astype(BF16)
    flat_ref[2 * R :] = filter_block(grad_filters_a[...]).astype(BF16)


def final_kernel(
    atoms,
    scalars, got, got_vec, features, stat, gain_ref, cot_f, cot_v, back_ref, mask,
    grad_feat, grad_vec, grad_pos, small_ref,
):
    chan_first = pl.multiple_of(scalars[1], R)
    whole_gain = column(gain_ref[...])
    gain = whole_gain[:R]
    for f in range(1, H // R):
        gain = jnp.where(chan_first == f * R, whole_gain[f * R : (f + 1) * R], gain)

    def summed(ref, rows):
        total = ref[0, rows].astype(F32)
        for f in range(1, ref.shape[0]):
            total = total + ref[f, rows].astype(F32)
        return total

    tops = summed(got, slice(R, R + EXTRAS))
    grad_normal = summed(got, slice(0, R))
    inv = stat[1:2]
    normed = (features[pl.ds(chan_first, R), :].astype(F32) - stat[0:1]) * inv
    inner = grad_normal * gain - tops[0:1] * (1.0 / H) - normed * (tops[1:2] * (1.0 / H))
    grad_feat[...] = cot_f[...].astype(F32) + inv * inner
    for d in range(3):
        part = summed(got_vec, slice(d * R, (d + 1) * R))
        grad_vec[d] = cot_v[d].astype(F32) + part + back_ref[d]
    exact = tops[2:9] + tops[9:16]
    grad_pos[...] = exact[:3]
    ones = jnp.ones((8, atoms), BF16)
    gains = dot_nt(ones, (grad_normal * normed).astype(BF16))
    biases = dot_nt(ones, grad_normal.astype(BF16))
    totals = jnp.sum(exact[3:7], axis=1, keepdims=True)
    real = jnp.sum(mask[...].astype(F32), axis=1, keepdims=True)
    numbers = jnp.concatenate([totals, real, jnp.zeros((3, 1), F32)], axis=0)
    small = jnp.concatenate([gains, biases, jnp.broadcast_to(numbers, (8, LANES))], axis=1)
    high = small.astype(BF16)
    small_ref[:8] = high.astype(F32)
    small_ref[8:] = small - high.astype(F32)


def unpack_kernel(
    share,
    got,
    g_gain, g_bias, g_query, g_key, g_value, g_vector, g_output, g_key_f, g_value_f, rms_ref,
):
    every = [got[n].astype(F32) for n in range(got.shape[0])]
    small = 0.0
    for x in every:
        small = small + x[share:]
    total = small[:8] + small[8:]
    g_gain[...] = total[0:1, :R]
    g_bias[...] = total[0:1, R : 2 * R]
    numbers = total[:, LANES : LANES + 1]
    size = jnp.where(lax.broadcasted_iota(jnp.int32, (8, 1), 0) < 2, 1.0, 3.0) * H
    rms = jnp.sqrt(numbers / (numbers[4:5] * size) + 1e-06)
    rms_ref[...] = jnp.broadcast_to(rms, (8, LANES)).T[:1, :8]
    order = [(g, p) for g in (g_vector, g_output) for p in range(3)]
    order += [(g_query, None), (g_key, None), (g_value, 0), ((g_key_f, None), (g_value_f, 0))]
    order += [(g_value, 1), (g_value, 2), ((g_value_f, 1), (g_value_f, 2))]
    begins = [0]
    for g, _ in order:
        begins.append(begins[-1] + (R // 2 if isinstance(g, tuple) else R))
    for n, x in enumerate(every):
        for (g, p), low, high in zip(order, begins[:-1], begins[1:]):
            first, last = max(low, n * share), min(high, (n + 1) * share)
            if first >= last:
                continue
            value = x[first - n * share : last - n * share]
            rows = slice(first - low, last - low)
            if not isinstance(g, tuple):
                put(g, p, rows, value)
                continue
            for h in (0, 1):
                down = slice(rows.start + h * R // 2, rows.stop + h * R // 2)
                at = h * LANES
                put(g[0], g[1], down, value[:, at : at + R])
                put(p[0], p[1], down, value[:, at + R : at + 2 * R])


def put(ref, p, rows, value):
    if p is None:
        ref[rows] = value
    else:
        ref[p, rows] = value


def everywhere(x, axis):
    count = lax.axis_size(axis)
    return lax.all_to_all(jnp.broadcast_to(x[None], (count,) + x.shape), axis, 0, 0)


def per_device(
    features, vectors, positions, atom_mask, neighbours, ln_gain, ln_bias,
    w_query, w_key, w_value, w_vector, w_output, w_key_filter, w_value_filter,
    cot_features, cot_vectors,
):
    channels = w_query.shape[1]
    atoms = features.shape[1]
    count = lax.axis_size("atoms")
    split = lax.axis_size("feat")
    chan_first = lax.axis_index("feat") * channels
    row_first = lax.axis_index("atoms") * atoms
    start = HALO - lax.rem(row_first, MOL)
    scalars = jnp.stack([start, chan_first, row_first]).astype(jnp.int32)
    molecules, rows_each, tall = edge_sizes(atoms)
    w_query, w_key = w_query.T, w_key.T
    w_value, w_vector, w_output = [jnp.swapaxes(w, 1, 2) for w in (w_value, w_vector, w_output)]
    mask = atom_mask.reshape(1, atoms)
    gain, bias = ln_gain.reshape(1, H), ln_bias.reshape(1, H)

    ends = halo_call(
        atoms,
        scalars,
        (features, vectors, cot_features, cot_vectors, neighbours, mask, positions),
    )
    low = lax.ppermute(ends[0], "atoms", [(i, i + 1) for i in range(count - 1)])
    high = lax.ppermute(ends[1], "atoms", [(i + 1, i) for i in range(count - 1)])

    inputs = (
        scalars, features, vectors, cot_features, cot_vectors, neighbours, mask, positions,
        low, high, gain, bias, w_query, w_key, w_value, w_vector, w_output,
    )
    rows, part, stat = pl.pallas_call(
        functools.partial(dense_kernel, atoms),
        out_shape=[
            jax.ShapeDtypeStruct((tall, 10 * LANES), BF16),
            jax.ShapeDtypeStruct((H, atoms + LANES), BF16),
            jax.ShapeDtypeStruct((8, atoms), F32),
        ],
        in_specs=[whole(pltpu.SMEM)] + [whole()] * (len(inputs) - 1),
        out_specs=[whole()] * 3,
        scratch_shapes=[
            pltpu.VMEM((LANES, H), BF16),
            pltpu.VMEM((LANES, H), BF16),
            pltpu.VMEM((LANES, H), BF16),
            pltpu.VMEM((3 * R, H), BF16),
            pltpu.VMEM((H, 3 * R), BF16),
        ],
        compiler_params=params(),
    )(*inputs)
    scalar_parts = lax.all_to_all(part.reshape(split, channels, atoms + LANES), "feat", 0, 0)

    kinds = shared_scratch(atoms)
    batch = OFFSETS * rows_each
    names = ["mask", "near", "near_last"] + ["tall"] * 3 + ["many", "stage2"]
    radial, geo = edge_call(
        geometry_kernel,
        atoms,
        (scalars, rows),
        (),
        [],
        [((SPAN, batch, 2 * LANES), BF16), ((SPAN, GEO, batch, LANES), BF16)],
        [kinds[name] for name in names],
    )
    names = ["weights", "weights", "near", "near_last", "stage4", "loose2"]
    names += ["loose_low", "pre", "grad_pre", "line", "wide2", "wide2f", "line4", "line1"]
    names += ["low"] * 4 + ["low"] * 4 + ["first"] * 4
    scalar_sum, grads_b, grad_filters_b, pull = edge_call(
        scalar_kernel,
        atoms,
        (scalars, rows, w_key_filter, w_value_filter[0], scalar_parts),
        (radial, geo),
        [
            ((R, atoms), BF16),
            ((3 * R, atoms), BF16),
            ((LANES, 2 * LANES), F32),
        ],
        [((SPAN, batch, LANES), BF16)],
        [kinds[name] for name in names],
    )
    gathered = lax.all_gather(scalar_sum, "feat", axis=0, tiled=True)

    inputs = (
        scalars, features, stat, vectors, cot_features, cot_vectors, gathered, grads_b,
        gain, bias, w_vector, w_output, grad_filters_b,
    )
    new_features, delta, squares, send_vec, flat_early = pl.pallas_call(
        functools.partial(layer_kernel, atoms),
        out_shape=[
            jax.ShapeDtypeStruct((R, atoms), BF16),
            jax.ShapeDtypeStruct((3, R, atoms), F32),
            jax.ShapeDtypeStruct((8, atoms), F32),
            jax.ShapeDtypeStruct((split, 3 * R, atoms), BF16),
            jax.ShapeDtypeStruct((EARLY, H), F32),
        ],
        in_specs=[whole(pltpu.SMEM)] + [whole()] * (len(inputs) - 1),
        out_specs=[whole()] * 5,
        scratch_shapes=[
            pltpu.VMEM((H, 3 * R), BF16),
            pltpu.VMEM((3 * R, H), BF16),
            pltpu.VMEM((3 * R, H), BF16),
        ],
        compiler_params=params(),
    )(*inputs)
    share = (EARLY + LATE) // count
    got_vec = lax.all_to_all(send_vec, "feat", 0, 0)

    names = ["weights", "near", "near_last", "stage8", "loose5"]
    names += ["pre", "grad_pre", "line", "line3"]
    names += ["low"] * 7 + ["low"] * 10 + ["first"] * 10
    rows, _ = lax.optimization_barrier((rows, squares))
    sums, back, grads_a, pos_a, grad_filters_a = edge_call(
        vector_kernel,
        atoms,
        (scalars, rows, w_value_filter[1], w_value_filter[2]),
        (radial, geo, pull),
        [
            ((3, R, atoms), F32),
            ((3, R, atoms), F32),
            ((2 * R, atoms), BF16),
            ((8, atoms), F32),
            ((LANES, 2 * LANES), F32),
        ],
        [],
        [kinds[name] for name in names],
    )

    delta, got_vec = lax.optimization_barrier((delta, got_vec))
    inputs = (
        scalars, features, stat, vectors, delta, squares, sums, grads_b, grads_a, pos_a,
        mask, gain, bias, w_query, w_key, w_value, grad_filters_a,
    )
    new_vectors, send, flat_late = pl.pallas_call(
        functools.partial(normal_kernel, atoms),
        out_shape=[
            jax.ShapeDtypeStruct((3, R, atoms), BF16),
            jax.ShapeDtypeStruct((split, R + EXTRAS, atoms), BF16),
            jax.ShapeDtypeStruct((LATE, H), BF16),
        ],
        in_specs=[whole(pltpu.SMEM)] + [whole()] * (len(inputs) - 1),
        out_specs=[whole()] * 3,
        scratch_shapes=[pltpu.VMEM((H, 5 * R), BF16), pltpu.VMEM((2 * R, H), F32)],
        compiler_params=params(),
    )(*inputs)
    got = lax.all_to_all(send, "feat", 0, 0)
    flat = jnp.concatenate([flat_early.astype(BF16), flat_late], axis=0)
    shares = lax.all_to_all(flat.reshape(count, share, H), "atoms", 0, 0)

    inputs = (
        scalars, got, got_vec, features, stat, gain, cot_features, cot_vectors, back, mask,
    )
    grad_features, grad_vectors, grad_positions, small = pl.pallas_call(
        functools.partial(final_kernel, atoms),
        out_shape=[
            jax.ShapeDtypeStruct((R, atoms), F32),
            jax.ShapeDtypeStruct((3, R, atoms), F32),
            jax.ShapeDtypeStruct((3, atoms), F32),
            jax.ShapeDtypeStruct((16, H), F32),
        ],
        in_specs=[whole(pltpu.SMEM)] + [whole()] * (len(inputs) - 1),
        out_specs=[whole()] * 4,
        compiler_params=params(),
    )(*inputs)
    mine = jnp.concatenate([jnp.sum(shares.astype(F32), axis=0), small], axis=0).astype(BF16)
    every = everywhere(mine, "atoms")
    shapes = [
        (1, R), (1, R), (R, H), (R, H), (3, R, H), (3, R, H), (3, R, H), (R, R), (3, R, R), (1, 8),
    ]
    grads = pl.pallas_call(
        functools.partial(unpack_kernel, share),
        out_shape=[jax.ShapeDtypeStruct(shape, F32) for shape in shapes],
        in_specs=[whole()],
        out_specs=[whole()] * len(shapes),
        compiler_params=params(),
    )(every)
    return (
        new_features,
        new_vectors,
        grad_features,
        grad_vectors,
        grad_positions,
        grads[0].reshape(R),
        grads[1].reshape(R),
        grads[2].T,
        grads[3].T,
        jnp.swapaxes(grads[4], 1, 2),
        jnp.swapaxes(grads[5], 1, 2),
        jnp.swapaxes(grads[6], 1, 2),
        grads[7],
        grads[8],
        grads[9][0, :4],
    )


def solution(mesh):
    in_specs = (
        P(None, "atoms"),
        P(None, None, "atoms"),
        P(None, "atoms"),
        P("atoms"),
        P(None, "atoms"),
        P(),
        P(),
        P(None, "feat"),
        P(None, "feat"),
        P(None, None, "feat"),
        P(None, None, "feat"),
        P(None, None, "feat"),
        P(None, "feat"),
        P(None, None, "feat"),
        P("feat", "atoms"),
        P(None, "feat", "atoms"),
    )
    out_specs = (
        P("feat", "atoms"),
        P(None, "feat", "atoms"),
        P("feat", "atoms"),
        P(None, "feat", "atoms"),
        P(None, "atoms"),
        P("feat"),
        P("feat"),
        P(None, "feat"),
        P(None, "feat"),
        P(None, None, "feat"),
        P(None, None, "feat"),
        P(None, None, "feat"),
        P(None, "feat"),
        P(None, None, "feat"),
        P(),
    )
    return jax.shard_map(
        per_device, mesh=mesh, in_specs=in_specs, out_specs=out_specs, check_vma=False
    )
```

profile of v0, /device:TPU:0, one launch (start us, length us, event | category | flops | bytes accessed | tf_op | source)
XLA Modules:
  0.0 200.0 jit_solution(10482078207350783545)
XLA Ops:
  0.7 0.6 pad_add_fusion.scalars
  1.2 0.0 copy-start.7
  1.2 2.1 %shard_map.271 = (bf16[352,128]{1,0:T(8,128)(2,1)}, bf16[352,128]{1,0:T(8,128)(2,1)}) custom-call(s32[3]{0:T(128)} %pad_add_fusion.scalars, bf16[256,1024]{1,0:T(8,128)(2,1)} %features.7, bf16[3,256,1024]{2,1,0:T(8,128)(2,1)} %vectors.5, bf16[64,1024]{1,0:T(8,128)(2,1)} %cot_f.5, bf16[3,64,1024]{2,1,0:T(8,128)(2,1)} %cot_v.5, s32[32,1024]{1,0:T(8,128)} %neighbours.1, ...), custom_call_target="tpu_custom_call" | custom-call | tf_op jit(solution)/shard_map/pallas_call | solution.py:695
  3.3 4.8 %collective-permute-start = (bf16[352,128]{1,0:T(8,128)(2,1)}, bf16[352,128]{1,0:T(8,128)(2,1)S(1)}, u32[]{:S(2)}, u32[]{:S(2)}) collective-permute-start(bf16[352,128]{1,0:T(8,128)(2,1)} %get-tuple-element.56), channel_id=1, source_target_pairs={{0,4},{4,8},{8,12},{12,16},{16,20},{20,24},{24,28},{1,5},{5,9},{9,... | collective-permute-start | bytes 270344 | tf_op jit(solution)/shard_map/ppermute | solution.py:1072
  8.2 1.3 collective-permute-start.1
  9.5 0.0 copy-done.7
  9.5 0.6 slice_bitcast_fusion
  10.1 0.5 collective-permute-done.low_ref
  10.6 0.0 copy-start.4
  10.6 4.2 %collective-permute-done.1.high_ref = bf16[352,128]{1,0:T(8,128)(2,1)S(1)} collective-permute-done((bf16[352,128]{1,0:T(8,128)(2,1)}, bf16[352,128]{1,0:T(8,128)(2,1)S(1)}, u32[]{:S(2)}, u32[]{:S(2)}) %collective-permute-start.1) | collective-permute-done | bytes 90144 | tf_op jit(solution)/shard_map/ppermute | solution.py:1073
  14.8 0.0 copy-start.5
  14.8 0.0 copy-done.4
  14.8 0.6 copy-done.5
  15.4 7.8 %shard_map.272 = (bf16[1120,1280]{1,0:T(8,128)(2,1)}, bf16[256,1152]{1,0:T(8,128)(2,1)}, f32[8,1024]{1,0:T(8,128)}) custom-call(s32[3]{0:T(128)} %pad_add_fusion.scalars, bf16[256,1024]{1,0:T(8,128)(2,1)} %features.7, bf16[3,256,1024]{2,1,0:T(8,128)(2,1)} %vectors.5, bf16[64,1024]{1,0:T(8,128)(2,1)} %cot_f.5, bf16[3,64,1024]{2,1,0:T(8,128)(2,1)} %cot_v.5, ...), custom_call_target="tpu_custom_call" | custom-call | tf_op jit(solution)/shard_map/pallas_call | solution.py:1079
  23.3 3.5 %all-to-all-start = ((bf16[4,64,1152]{2,1,0:T(8,128)(2,1)}), bf16[4,64,1152]{2,1,0:T(8,128)(2,1)S(1)}, u32[]{:S(2)}, u32[]{:S(2)}) async-start(bf16[4,64,1152]{2,1,0:T(8,128)(2,1)} %bitcast.28), calls=%async_computation | async-start | bytes 1179648 | tf_op jit(solution)/shard_map/all_to_all | solution.py:1097
  26.8 21.7 %shard_map.273 = (bf16[5,1568,256]{2,1,0:T(8,128)(2,1)}, bf16[5,10,1568,128]{3,2,1,0:T(8,128)(2,1)}) custom-call(s32[3]{0:T(128)} %pad_add_fusion.scalars, bf16[1120,1280]{1,0:T(8,128)(2,1)} %get-tuple-element.71.rows_ref), custom_call_target="tpu_custom_call" | custom-call | flops 20000000000 | bytes 40000000 | tf_op jit(solution)/shard_map/pallas_call | solution.py:603
  48.5 0.0 all-to-all-done.scalar_parts
  48.5 0.0 copy-start.3
  48.5 0.8 copy-done.3
  49.3 34.5 %shard_map.274 = (bf16[64,1024]{1,0:T(8,128)(2,1)}, bf16[192,1024]{1,0:T(8,128)(2,1)}, f32[128,256]{1,0:T(8,128)}, bf16[5,1568,128]{2,1,0:T(8,128)(2,1)}) custom-call(s32[3]{0:T(128)} %pad_add_fusion.scalars, bf16[1120,1280]{1,0:T(8,128)(2,1)} %get-tuple-element.71.rows_ref, bf16[64,64]{1,0:T(8,128)(2,1)} %filter_1.1, ...), custom_call_target="tpu_custom_call" | custom-call | flops 20000000000 | bytes 40000000 | tf_op jit(solution)/shard_map/pallas_call | solution.py:603
  83.8 9.5 %all_gather.3.gathered = bf16[256,1024]{1,0:T(8,128)(2,1)} all-gather(bf16[64,1024]{1,0:T(8,128)(2,1)} %get-tuple-element.63), channel_id=1, replica_groups=mesh['atoms'=8,'feat'=4] {'feat'}, dimensions={0}, use_global_device_ids=true | all-gather | bytes 655360 | tf_op jit(solution)/shard_map/all_gather | solution.py:1127
  93.3 7.0 %shard_map.275 = (bf16[64,1024]{1,0:T(8,128)(2,1)}, f32[3,64,1024]{2,1,0:T(8,128)}, f32[8,1024]{1,0:T(8,128)}, bf16[4,192,1024]{2,1,0:T(8,128)(2,1)}, f32[608,256]{1,0:T(8,128)}) custom-call(s32[3]{0:T(128)} %pad_add_fusion.scalars, bf16[256,1024]{1,0:T(8,128)(2,1)} %features.7, f32[8,1024]{1,0:T(8,128)} %get-tuple-element.58.stat, ...), custom_call_target="tpu_custom_call" | custom-call | tf_op jit(solution)/shard_map/pallas_call | solution.py:1133
  100.3 3.7 %all-to-all-start.1 = ((bf16[4,192,1024]{2,1,0:T(8,128)(2,1)}), bf16[4,192,1024]{2,1,0:T(8,128)(2,1)S(1)}, u32[]{:S(2)}, u32[]{:S(2)}) async-start(bf16[4,192,1024]{2,1,0:T(8,128)(2,1)} %get-tuple-element.68), calls=%async_computation.1 | async-start | bytes 3145728 | tf_op jit(solution)/shard_map/all_to_all | solution.py:1152
  104.1 39.6 %shard_map.276 = (f32[3,64,1024]{2,1,0:T(8,128)}, f32[3,64,1024]{2,1,0:T(8,128)}, bf16[128,1024]{1,0:T(8,128)(2,1)}, f32[8,1024]{1,0:T(8,128)}, f32[128,256]{1,0:T(8,128)}) custom-call(s32[3]{0:T(128)} %pad_add_fusion.scalars, bf16[1120,1280]{1,0:T(8,128)(2,1)} %get-tuple-element.71.rows_ref, bf16[64,64]{1,0:T(8,128)(2,1)} %get-tuple-element.99.filter_1, ...), custom_call_target="tpu_custom_call" | custom-call | flops 20000000000 | bytes 40000000 | tf_op jit(solution)/shard_map/pallas_call | solution.py:603
  143.7 0.0 all-to-all-done.1.got_vec
  143.7 0.0 copy-start
  143.7 0.0 copy-start.2
  143.7 5.7 %shard_map.277 = (bf16[3,64,1024]{2,1,0:T(8,128)(2,1)}, bf16[4,80,1024]{2,1,0:T(8,128)(2,1)}, bf16[160,256]{1,0:T(8,128)(2,1)}) custom-call(s32[3]{0:T(128)} %pad_add_fusion.scalars, bf16[256,1024]{1,0:T(8,128)(2,1)} %features.7, f32[8,1024]{1,0:T(8,128)} %get-tuple-element.58.stat, bf16[3,256,1024]{2,1,0:T(8,128)(2,1)} %vectors.5, ...), custom_call_target="tpu_custom_call" | custom-call | tf_op jit(solution)/shard_map/pallas_call | solution.py:1179
  149.4 0.0 copy-done
  149.4 0.0 copy-start.6
  149.4 3.6 %all-to-all-start.2 = ((bf16[4,80,1024]{2,1,0:T(8,128)(2,1)}), bf16[4,80,1024]{2,1,0:T(8,128)(2,1)S(1)}, u32[]{:S(2)}, u32[]{:S(2)}) async-start(bf16[4,80,1024]{2,1,0:T(8,128)(2,1)} %get-tuple-element.78), calls=%async_computation.2 | async-start | bytes 1310720 | tf_op jit(solution)/shard_map/all_to_all | solution.py:1191
  153.0 0.0 copy-done.2
  153.1 0.0 copy-done.6
  153.1 0.8 pad_maximum_fusion
  153.9 9.4 %all-to-all-done.2.got = bf16[4,80,1024]{2,1,0:T(8,128)(2,1)S(1)} async-done(((bf16[4,80,1024]{2,1,0:T(8,128)(2,1)}), bf16[4,80,1024]{2,1,0:T(8,128)(2,1)S(1)}, u32[]{:S(2)}, u32[]{:S(2)}) %all-to-all-start.2) | async-done | bytes 655392 | tf_op jit(solution)/shard_map/all_to_all | solution.py:1191
  163.3 0.0 copy-start.1
  163.3 5.8 %all-to-all-start.3 = ((bf16[8,96,256]{2,1,0:T(8,128)(2,1)}), bf16[8,96,256]{2,1,0:T(8,128)(2,1)S(1)}, u32[]{:S(2)}, u32[]{:S(2)}) async-start(bf16[8,96,256]{2,1,0:T(8,128)(2,1)} %bitcast.15), calls=%async_computation.3 | async-start | bytes 786432 | tf_op jit(solution)/shard_map/all_to_all | solution.py:1193
  169.1 0.0 copy-done.1
  169.1 3.7 %shard_map.278 = (f32[64,1024]{1,0:T(8,128)}, f32[3,64,1024]{2,1,0:T(8,128)}, f32[3,1024]{1,0:T(4,128)}, f32[16,256]{1,0:T(8,128)}) custom-call(s32[3]{0:T(128)} %pad_add_fusion.scalars, bf16[4,80,1024]{2,1,0:T(8,128)(2,1)} %copy-done.1, bf16[4,192,1024]{2,1,0:T(8,128)(2,1)} %copy-done, bf16[256,1024]{1,0:T(8,128)(2,1)} %features.7, ...), custom_call_target="tpu_custom_call" | custom-call | tf_op jit(solution)/shard_map/pallas_call | solution.py:1198
  172.7 0.7 convert.7
  173.5 7.1 %all-to-all-done.3 = bf16[8,96,256]{2,1,0:T(8,128)(2,1)S(1)} async-done(((bf16[8,96,256]{2,1,0:T(8,128)(2,1)}), bf16[8,96,256]{2,1,0:T(8,128)(2,1)S(1)}, u32[]{:S(2)}, u32[]{:S(2)}) %all-to-all-start.3) | async-done | bytes 393248 | tf_op jit(solution)/shard_map/all_to_all | solution.py:1193
  180.6 0.1 reduce
  180.7 16.2 %all_to_all.25.got = bf16[8,112,256]{2,1,0:T(8,128)(2,1)} all-to-all(bf16[8,112,256]{2,1,0:T(8,128)(2,1)S(1)} %broadcast_in_dim.2), channel_id=1, replica_groups=mesh['atoms'=8,'feat'=4] {'atoms'}, dimensions={0} | all-to-all | bytes 917504 | tf_op jit(solution)/shard_map/all_to_all | solution.py:1045
  196.9 2.0 shard_map.279
  198.9 1.1 slice_bitcast_fusion.3
  (3 shorter events, 0.1 us)
Async XLA Ops:
  1.2 8.2 %copy-start.7 = (bf16[3,64,64]{2,1,0:T(8,128)(2,1)S(1)}, bf16[3,64,64]{2,1,0:T(8,128)(2,1)}, u32[]{:S(2)}) copy-start(bf16[3,64,64]{2,1,0:T(8,128)(2,1)} %param.29) | copy-start | bytes 73732
  3.3 7.3 %collective-permute-start = (bf16[352,128]{1,0:T(8,128)(2,1)}, bf16[352,128]{1,0:T(8,128)(2,1)S(1)}, u32[]{:S(2)}, u32[]{:S(2)}) collective-permute-start(bf16[352,128]{1,0:T(8,128)(2,1)} %get-tuple-element.56), channel_id=1, source_target_pairs={{0,4},{4,8},{8,12},{12,16},{16,20},{20,24},{24,28},{1,5},{5,9},{9,... | collective-permute-start | bytes 270344 | tf_op jit(solution)/shard_map/ppermute | solution.py:1072
  8.2 6.6 %collective-permute-start.1 = (bf16[352,128]{1,0:T(8,128)(2,1)}, bf16[352,128]{1,0:T(8,128)(2,1)S(1)}, u32[]{:S(2)}, u32[]{:S(2)}) collective-permute-start(bf16[352,128]{1,0:T(8,128)(2,1)} %get-tuple-element.57), channel_id=1, source_target_pairs={{4,0},{8,4},{12,8},{16,12},{20,16},{24,20},{28,24},{5,1},{9,5},{13... | collective-permute-start | bytes 270344 | tf_op jit(solution)/shard_map/ppermute | solution.py:1073
  10.6 4.2 %copy-start.4 = (bf16[352,128]{1,0:T(8,128)(2,1)}, bf16[352,128]{1,0:T(8,128)(2,1)S(1)}, u32[]{:S(2)}) copy-start(bf16[352,128]{1,0:T(8,128)(2,1)S(1)} %collective-permute-done.low_ref) | copy-start | bytes 270340
  14.8 0.6 copy-start.5
  23.3 25.2 %all-to-all-start = ((bf16[4,64,1152]{2,1,0:T(8,128)(2,1)}), bf16[4,64,1152]{2,1,0:T(8,128)(2,1)S(1)}, u32[]{:S(2)}, u32[]{:S(2)}) async-start(bf16[4,64,1152]{2,1,0:T(8,128)(2,1)} %bitcast.28), calls=%async_computation | async-start | bytes 1179648 | tf_op jit(solution)/shard_map/all_to_all | solution.py:1097
  48.5 0.8 copy-start.3
  100.3 43.3 %all-to-all-start.1 = ((bf16[4,192,1024]{2,1,0:T(8,128)(2,1)}), bf16[4,192,1024]{2,1,0:T(8,128)(2,1)S(1)}, u32[]{:S(2)}, u32[]{:S(2)}) async-start(bf16[4,192,1024]{2,1,0:T(8,128)(2,1)} %get-tuple-element.68), calls=%async_computation.1 | async-start | bytes 3145728 | tf_op jit(solution)/shard_map/all_to_all | solution.py:1152
  143.7 5.7 %copy-start = (bf16[4,192,1024]{2,1,0:T(8,128)(2,1)}, bf16[4,192,1024]{2,1,0:T(8,128)(2,1)S(1)}, u32[]{:S(2)}) copy-start(bf16[4,192,1024]{2,1,0:T(8,128)(2,1)S(1)} %all-to-all-done.1.got_vec) | copy-start | bytes 4718596
  143.7 9.4 %copy-start.2 = (f32[608,256]{1,0:T(8,128)S(1)}, f32[608,256]{1,0:T(8,128)}, u32[]{:S(2)}) copy-start(f32[608,256]{1,0:T(8,128)} %get-tuple-element.84) | copy-start | bytes 1867780
  149.4 3.7 %copy-start.6 = (bf16[160,256]{1,0:T(8,128)(2,1)S(1)}, bf16[160,256]{1,0:T(8,128)(2,1)}, u32[]{:S(2)}) copy-start(bf16[160,256]{1,0:T(8,128)(2,1)} %get-tuple-element.85) | copy-start | bytes 245764
  149.4 13.8 %all-to-all-start.2 = ((bf16[4,80,1024]{2,1,0:T(8,128)(2,1)}), bf16[4,80,1024]{2,1,0:T(8,128)(2,1)S(1)}, u32[]{:S(2)}, u32[]{:S(2)}) async-start(bf16[4,80,1024]{2,1,0:T(8,128)(2,1)} %get-tuple-element.78), calls=%async_computation.2 | async-start | bytes 1310720 | tf_op jit(solution)/shard_map/all_to_all | solution.py:1191
  163.3 5.8 %copy-start.1 = (bf16[4,80,1024]{2,1,0:T(8,128)(2,1)}, bf16[4,80,1024]{2,1,0:T(8,128)(2,1)S(1)}, u32[]{:S(2)}) copy-start(bf16[4,80,1024]{2,1,0:T(8,128)(2,1)S(1)} %all-to-all-done.2.got) | copy-start | bytes 1966084
  163.3 17.3 %all-to-all-start.3 = ((bf16[8,96,256]{2,1,0:T(8,128)(2,1)}), bf16[8,96,256]{2,1,0:T(8,128)(2,1)S(1)}, u32[]{:S(2)}, u32[]{:S(2)}) async-start(bf16[8,96,256]{2,1,0:T(8,128)(2,1)} %bitcast.15), calls=%async_computation.3 | async-start | bytes 786432 | tf_op jit(solution)/shard_map/all_to_all | solution.py:1193
where the time goes:
time: 201 us; the launch traced here: 200 us
  Pallas kernels  124 us (62%)
  blocking collectives  25.7 us (13%)
  starting transfers between devices  22.8 us (11%)
  waiting for transfers between devices  21.2 us (11%)
  local copies, waits for them, and re-layouts  3.23 us (2%)
  other arithmetic  2.18 us (1%)
    pallas_call x3, Pallas kernels, edge_call(): pl.pallas_call(functools.partial(kernel, molecules, rows, atoms), grid=(S...  95.8 us
    all_to_all x1, blocking collectives, everywhere(): lax.all_to_all(jnp.broadcast_to(x[None], (count,) + x.shape), axis, 0, 0)  16.2 us
    all_gather x1, blocking collectives, per_device(): gathered = lax.all_gather(scalar_sum, 'feat', axis=0, tiled=True)  9.48 us
    all_to_all x1, waiting for transfers between devices, per_device(): got = lax.all_to_all(send, 'feat', 0, 0)  9.38 us
    pallas_call x1, Pallas kernels, per_device(): pl.pallas_call(functools.partial(dense_kernel, atoms), out_shape=[jax.Sha...  7.84 us
    all_to_all x1, waiting for transfers between devices, per_device(): shares = lax.all_to_all(flat.reshape(count, share, H), 'atoms', 0, 0)  7.12 us
    pallas_call x1, Pallas kernels, per_device(): pl.pallas_call(functools.partial(layer_kernel, atoms), out_shape=[jax.Sha...  7.02 us
    all_to_all x1, starting transfers between devices, per_device(): shares = lax.all_to_all(flat.reshape(count, share, H), 'atoms', 0, 0)  5.79 us
  transfers between devices with their start and end apart: 6, of which 4 were waited for; matrix products, arithmetic and copies ran while one was open for 1% of the time, Pallas kernels for 32%

commit v1 on v0

--- a/solution.py
+++ b/solution.py
@@ -27,7 +27,7 @@
 SUB = 16
 LANES = 128
 
-W01, W2V2, C01, C2_COUNT, POS, QK, V0_COUNT, V12, VEC01, VEC2 = range(10)
+W01, W2V2, C01, C2_COUNT, POS, QK, V0, V12, VEC01, VEC2 = range(10)
 GROUP_ROWS = 352
 EARLY = 9 * R + R // 2
 LATE = 2 * R + R // 2
@@ -80,34 +80,67 @@
         yield first, width, pl.ds(base, WINDOW), ones
 
 
-def spread(source, lanes, stage, blocks, distances, start):
+def both_ways(given):
+    top, bottom = [], []
+    for n in range(given.shape[1] // LANES):
+        x = given[:, n * LANES : (n + 1) * LANES].astype(F32)
+        y = pltpu.roll(x, R, 1)
+        low = lax.broadcasted_iota(jnp.int32, x.shape, 1) < R
+        top += [jnp.where(low, x, 0.0), jnp.where(low, y, 0.0)]
+        bottom += [jnp.where(low, 0.0, y), jnp.where(low, 0.0, x)]
+    return jnp.concatenate(
+        [jnp.concatenate(top, axis=1), jnp.concatenate(bottom, axis=1)], axis=0
+    ).astype(BF16)
+
+
+def spread(source, targets, blocks, distances, start, extra=None):
+    waiting = None
     for first, width, here, ones in windows(blocks, distances, start, source.shape[0]):
-        given = source[here, lanes]
-        a, b = dot(ones[0], given), dot(ones[1], given)
-        low = lax.broadcasted_iota(jnp.int32, (a.shape[0], LANES), 1) < R
-        for n in range(a.shape[1] // LANES):
-            left, right = a[:, n * LANES : (n + 1) * LANES], b[:, n * LANES : (n + 1) * LANES]
-            one = jnp.where(low, left, pltpu.roll(right, R, 1))
-            two = jnp.where(low, pltpu.roll(left, R, 1), right)
-            stage[2 * n, :, first : first + width] = one.reshape(STEPS, width, LANES)
-            stage[2 * n + 1, :, first : first + width] = two.reshape(STEPS, width, LANES)
-
-
-def spread_positions(source, lanes, targets, blocks, distances, start):
-    row = lax.broadcasted_iota(jnp.int32, (LANES, 3 * LANES), 0)
-    lane = lax.broadcasted_iota(jnp.int32, (LANES, 3 * LANES), 1)
+        given = source[here, :]
+        ones = jnp.concatenate(ones, axis=1)
+        out = dot(ones, both_ways(given)).reshape(STEPS, width, 2 * given.shape[1])
+        if extra is not None:
+            extra(ones, here, first, width)
+        if waiting is not None:
+            first, out = waiting[0], jnp.concatenate([waiting[1], out], axis=1)
+            waiting = None
+        elif width % SUB:
+            waiting = (first, out)
+            continue
+        for n, target in enumerate(targets):
+            if target is not None:
+                value = out[:, :, n * LANES : (n + 1) * LANES]
+                target[:, first : first + out.shape[1]] = value.astype(target.dtype)
+
+
+def position_spreader(source, targets):
+    row = lax.broadcasted_iota(jnp.int32, (2 * LANES, 3 * LANES), 0)
+    lane = lax.broadcasted_iota(jnp.int32, (2 * LANES, 3 * LANES), 1)
     axis = jnp.where(lane >= 2 * LANES, 2, jnp.where(lane >= LANES, 1, 0))
-    mine = (row >= 3 * axis) & (row < 3 * axis + 3)
+    part = jnp.where(row >= LANES, row - LANES, row)
+    mine = (part >= 3 * axis) & (part < 3 * axis + 3)
     low = lane - axis * LANES < R
-    wide = [jnp.where(mine & (low == (r == 0)), 1.0, 0.0).astype(BF16) for r in (0, 1)]
-    for first, width, here, ones in windows(blocks, distances, start, source.shape[0]):
-        given = source[here, lanes]
-        total = 0.0
-        for r in (0, 1):
-            total = total + dot(dot(ones[r], given).astype(BF16), wide[r])
+    wide = jnp.where(mine & (low == (row < LANES)), 1.0, 0.0).astype(BF16)
+
+    def place(ones, here, first, width):
+        given = source[here, :]
+        found = [dot(ones[:, r * WINDOW : (r + 1) * WINDOW], given) for r in (0, 1)]
+        total = dot(jnp.concatenate(found, axis=1).astype(BF16), wide)
         for d, target in enumerate(targets):
             value = total[:, d * LANES : (d + 1) * LANES]
             target[:, first : first + width] = value.reshape(STEPS, width, LANES)
+
+    return place
+
+
+def assemble(target, own_ref, halo_ref, lanes, at=0):
+    atoms, tall, size = own_ref.shape[0], target.shape[0], lanes.stop - lanes.start
+    there = slice(at, at + size)
+    target[HALO : HALO + atoms, there] = own_ref[:, lanes]
+    target[:HALO, there] = halo_ref[:HALO, lanes]
+    end = 2 * HALO + atoms
+    target[HALO + atoms : end, there] = halo_ref[HALO : 2 * HALO, lanes]
+    target[end:, there] = jnp.zeros((tall - end, size), BF16)
 
 
 def collect(sources, target, blocks, distances, start):
@@ -287,7 +320,8 @@
 
 def geometry_kernel(
     molecules, rows, atoms,
-    scalars, rows_ref, radial_out, geo_out, owned, near, near_last, px, py, pz, many, stage,
+    scalars, own_ref, halo_ref, radial_out, geo_out,
+    owned, near, near_last, px, py, pz, many, count, all_pos, all_count,
 ):
     t = pl.program_id(0)
     start = scalars[0]
@@ -299,20 +333,20 @@
         row_masks(owned, start, blocks, atoms)
         set_distances(near, blocks[0][1], blocks[0][2])
         set_distances(near_last, blocks[-1][1], blocks[-1][2])
-        lanes = slice(POS * LANES, (POS + 1) * LANES)
-        spread_positions(rows_ref, lanes, (px, py, pz), blocks, distances, start)
-        lanes = slice(C2_COUNT * LANES, (C2_COUNT + 1) * LANES)
-        spread(rows_ref, lanes, stage, blocks, distances, start)
-        set_multiplicities(stage.at[1], many, blocks, rows)
+        assemble(all_pos, own_ref, halo_ref, slice(POS * LANES, (POS + 1) * LANES))
+        assemble(all_count, own_ref, halo_ref, slice(C2_COUNT * LANES, (C2_COUNT + 1) * LANES))
+        extra = position_spreader(all_pos, (px, py, pz))
+        spread(all_count, (None, count), blocks, distances, start, extra)
+        set_multiplicities(count, many, blocks, rows)
 
     geometry((px, py, pz), many, t, rows, owned, radial_out.at[0], geo_out.at[0])
 
 
 def vector_kernel(
     molecules, rows, atoms,
-    scalars, rows_ref, filter_1, filter_2, radial_in, geo_in, pull_in,
+    scalars, own_ref, halo_ref, filter_1, filter_2, radial_in, geo_in, pull_in,
     sums_ref, back_ref, grads_ref, pos_out, grad_w_ref,
-    weights_ref, near, near_last, stage, loose, pre, grad_pre,
+    weights_ref, near, near_last, all_rows, loose, pre, grad_pre,
     grad_radial, grad_ways,
     w0, w1, w2, v2, c0, c1, c2,
     s0, s1, s2, a0, a1, a2, gv, gx, gy, gz,
@@ -332,10 +366,8 @@
         set_filters(weights_ref, filter_1, filter_2)
         set_distances(near, blocks[0][1], blocks[0][2])
         set_distances(near_last, blocks[-1][1], blocks[-1][2])
-        lanes = slice(W01 * LANES, (C2_COUNT + 1) * LANES)
-        spread(rows_ref, lanes, stage, blocks, distances, start)
-        for n, target in enumerate((w0, w1, w2, v2, c0, c1, c2)):
-            target[...] = stage[n].astype(BF16)
+        assemble(all_rows, own_ref, halo_ref, slice(W01 * LANES, (C2_COUNT + 1) * LANES))
+        spread(all_rows, (w0, w1, w2, v2, c0, c1, c2), blocks, distances, start)
         for total in (s0, s1, s2, a0, a1, a2, gv, gx, gy, gz):
             total[...] = jnp.zeros(total.shape, BF16)
         grad_w_ref[...] = jnp.zeros(grad_w_ref.shape, F32)
@@ -420,7 +452,7 @@
         grads_ref[R:] = both[R:].astype(BF16)
 
         def kept(n):
-            return rows_ref[own, n * LANES : (n + 1) * LANES].astype(F32)
+            return own_ref[:, n * LANES : (n + 1) * LANES].astype(F32)
 
         v12 = kept(V12)
         v11 = jnp.where(low, v12, pltpu.roll(v12, R, 1))
@@ -443,9 +475,9 @@
 
 def scalar_kernel(
     molecules, rows, atoms,
-    scalars, rows_ref, filter_1, filter_2, scalar_parts, radial_in, geo_in,
+    scalars, own_ref, halo_ref, filter_1, filter_2, scalar_parts, radial_in, geo_in,
     sum_ref, grads_ref, grad_w_ref, pull_out,
-    weights_ref, heads_ref, near, near_last, stage, loose, loose_low, pre,
+    weights_ref, heads_ref, near, near_last, all_rows, loose, pre,
     grad_pre, grad_radial, products, sums, gates, bends,
     q, key, v0, gs,
     ss, gq, gk, g0,
@@ -466,21 +498,20 @@
         heads_ref[...] = jnp.where(row // HEAD == lane // HEAD, 1.0, 0.0).astype(BF16)
         set_distances(near, blocks[0][1], blocks[0][2])
         set_distances(near_last, blocks[-1][1], blocks[-1][2])
-        lanes = slice(QK * LANES, (V0_COUNT + 1) * LANES)
-        spread(rows_ref, lanes, stage, blocks, distances, start)
-        for n, target in enumerate((q, key, v0)):
-            target[...] = stage[n].astype(BF16)
+        assemble(all_rows, own_ref, halo_ref, slice(QK * LANES, (V0 + 1) * LANES))
         summed = scalar_parts[0].astype(F32)
         for f in range(1, scalar_parts.shape[0]):
             summed = summed + scalar_parts[f].astype(F32)
-        summed = jnp.concatenate([summed, jnp.zeros_like(summed)], axis=0).T.astype(BF16)
-        loose_low[own] = summed[:atoms]
-        loose_low[:HALO] = summed[atoms : atoms + HALO]
-        loose_low[HALO + atoms : 2 * HALO + atoms] = summed[atoms + HALO : atoms + 2 * HALO]
-        end = 2 * HALO + atoms
-        loose_low[end:] = jnp.zeros((loose_low.shape[0] - end, LANES), BF16)
-        spread(loose_low, slice(None), stage, blocks, distances, start)
-        gs[...] = stage[0].astype(BF16)
+        summed = jnp.concatenate([jnp.zeros_like(summed), summed], axis=0).T
+        here = slice(LANES, 2 * LANES)
+        for low, high, at in (
+            (HALO, HALO + atoms, 0),
+            (0, HALO, atoms),
+            (HALO + atoms, 2 * HALO + atoms, atoms + HALO),
+        ):
+            both = all_rows[low:high, here].astype(F32) + summed[at : at + high - low]
+            all_rows[low:high, here] = both.astype(BF16)
+        spread(all_rows, (q, key, v0, gs), blocks, distances, start)
         for total in (ss, gq, gk, g0):
             total[...] = jnp.zeros(total.shape, BF16)
         grad_w_ref[...] = jnp.zeros(grad_w_ref.shape, F32)
@@ -623,15 +654,14 @@
     return {
         "weights": ((2 * LANES, 2 * LANES), BF16),
         "many": ((SPAN, rows, LANES), F32),
-        "stage2": ((2, STEPS, rows, LANES), F32),
         "mask": ((rows, LANES), F32),
         "near": ((LANE_GROUPS, STEPS * blocks[0][1], WINDOW), jnp.int32),
         "near_last": ((LANE_GROUPS, STEPS * blocks[-1][1], WINDOW), jnp.int32),
-        "stage8": ((8, STEPS, rows, LANES), F32),
-        "stage4": ((4, STEPS, rows, LANES), F32),
+        "row1": ((tall, LANES), BF16),
+        "row2": ((tall, 2 * LANES), BF16),
+        "row4": ((tall, 4 * LANES), BF16),
         "loose5": ((tall, 5 * LANES), F32),
         "loose2": ((tall, 2 * LANES), F32),
-        "loose_low": ((tall, LANES), BF16),
         "tall": ((STEPS, rows, LANES), F32),
         "low": ((STEPS, rows, LANES), BF16),
         "first": ((SPAN, rows, LANES), F32),
@@ -713,15 +743,8 @@
     return centred * inv, mean, inv
 
 
-def dense_kernel(
-    atoms,
-    scalars, features, vectors, cot_f, cot_v, neighbours, mask, positions, low_ref, high_ref,
-    gain_ref, bias_ref, w_query, w_key, w_value, w_vector, w_output,
-    rows_ref, part_ref, stat_ref,
-    w_qk, w_v0, w_v12, w_vec_t, w_out,
-):
-    chan_first = pl.multiple_of(scalars[1], R)
-    row_first = scalars[2]
+def dense_block(gain_ref, bias_ref, w_query, w_key, w_value, w_vector, w_output, scratch):
+    w_qk, w_v0, w_v12, w_vec_t, w_out = scratch
     gain, bias = column(gain_ref[...]), column(bias_ref[...])
     w_qk[:R] = w_query[...]
     w_qk[R:] = w_key[...]
@@ -747,7 +770,7 @@
         low = lax.broadcasted_iota(jnp.int32, (width, LANES), 1) < R
         pairs = [None] * 10
         pairs[QK] = dot_nt(turned, w_qk[...])
-        pairs[V0_COUNT] = dot_nt(turned, w_v0[...]) + counts
+        pairs[V0] = dot_nt(turned, w_v0[...])
         v12 = dot_nt(turned, w_v12[...]).astype(BF16).astype(F32)
         v11 = jnp.where(low, v12, pltpu.roll(v12, R, 1))
         pairs[V12] = v12
@@ -767,6 +790,19 @@
         part = dot(w_out[...], grad_out)
         return [x.astype(BF16) for x in pairs], part.astype(BF16), mean, inv
 
+    return block
+
+
+def dense_kernel(
+    atoms,
+    scalars, features, vectors, cot_f, cot_v, neighbours, mask, positions,
+    gain_ref, bias_ref, w_query, w_key, w_value, w_vector, w_output,
+    rows_ref, part_ref, stat_ref, *scratch,
+):
+    chan_first = pl.multiple_of(scalars[1], R)
+    row_first = scalars[2]
+    weights = (w_query, w_key, w_value, w_vector, w_output)
+    block = dense_block(gain_ref, bias_ref, *weights, scratch)
     wide = 2 * LANES
 
     def step(b, _):
@@ -784,9 +820,8 @@
             diff.astype(F32),
             jnp.concatenate(places, axis=0),
         )
-        there = pl.ds(pl.multiple_of(HALO + at, 2 * SUB), wide)
         for n, pair in enumerate(pairs):
-            rows_ref[there, n * LANES : (n + 1) * LANES] = pair
+            rows_ref[here, n * LANES : (n + 1) * LANES] = pair
         part_ref[:, here] = part
         stat_ref[0:1, here] = mean
         stat_ref[1:2, here] = inv
@@ -794,6 +829,16 @@
 
     lax.fori_loop(0, atoms // wide, step, 0)
 
+
+def dense_halo_kernel(
+    atoms,
+    scalars, low_ref, high_ref, part_in, gain_ref, bias_ref,
+    w_query, w_key, w_value, w_vector, w_output,
+    rows_ref, part_ref, *scratch,
+):
+    chan_first = pl.multiple_of(scalars[1], R)
+    weights = (w_query, w_key, w_value, w_vector, w_output)
+    block = dense_block(gain_ref, bias_ref, *weights, scratch)
     lane = lax.broadcasted_iota(jnp.int32, (GROUP_ROWS, LANES), 1)
     packed_low, packed_high = low_ref[...].astype(F32), high_ref[...].astype(F32)
     groups = []
@@ -803,7 +848,6 @@
         b = pltpu.roll(packed_high, by, 1) if by else packed_high
         both = jnp.where(lane < HALO, a, jnp.where(lane < 2 * HALO, b, 0.0))
         groups.append(both)
-    pick_rows = lax.broadcasted_iota(jnp.int32, (H, LANES), 0)
     own_v, pos = [], []
     for d in range(3):
         g = groups[1 + d]
@@ -821,13 +865,9 @@
         groups[0][H + R :],
         jnp.concatenate(pos, axis=0),
     )
-    high = HALO + atoms
-    tall = rows_ref.shape[0]
     for n, pair in enumerate(pairs):
-        lanes = slice(n * LANES, (n + 1) * LANES)
-        rows_ref[:HALO, lanes] = pair[:HALO]
-        rows_ref[high : high + HALO, lanes] = pair[HALO : 2 * HALO]
-        rows_ref[high + HALO :, lanes] = jnp.zeros((tall - high - HALO, LANES), BF16)
+        rows_ref[:, n * LANES : (n + 1) * LANES] = pair
+    part_ref[:, :atoms] = part_in[...]
     part_ref[:, atoms:] = part
 
 
@@ -1072,49 +1112,65 @@
     low = lax.ppermute(ends[0], "atoms", [(i, i + 1) for i in range(count - 1)])
     high = lax.ppermute(ends[1], "atoms", [(i + 1, i) for i in range(count - 1)])
 
+    scratch = [
+        pltpu.VMEM((LANES, H), BF16),
+        pltpu.VMEM((LANES, H), BF16),
+        pltpu.VMEM((LANES, H), BF16),
+        pltpu.VMEM((3 * R, H), BF16),
+        pltpu.VMEM((H, 3 * R), BF16),
+    ]
+    weights = (gain, bias, w_query, w_key, w_value, w_vector, w_output)
     inputs = (
         scalars, features, vectors, cot_features, cot_vectors, neighbours, mask, positions,
-        low, high, gain, bias, w_query, w_key, w_value, w_vector, w_output,
-    )
+    ) + weights
     rows, part, stat = pl.pallas_call(
         functools.partial(dense_kernel, atoms),
         out_shape=[
-            jax.ShapeDtypeStruct((tall, 10 * LANES), BF16),
-            jax.ShapeDtypeStruct((H, atoms + LANES), BF16),
+            jax.ShapeDtypeStruct((atoms, 10 * LANES), BF16),
+            jax.ShapeDtypeStruct((H, atoms), BF16),
             jax.ShapeDtypeStruct((8, atoms), F32),
         ],
         in_specs=[whole(pltpu.SMEM)] + [whole()] * (len(inputs) - 1),
         out_specs=[whole()] * 3,
-        scratch_shapes=[
-            pltpu.VMEM((LANES, H), BF16),
-            pltpu.VMEM((LANES, H), BF16),
-            pltpu.VMEM((LANES, H), BF16),
-            pltpu.VMEM((3 * R, H), BF16),
-            pltpu.VMEM((H, 3 * R), BF16),
+        scratch_shapes=scratch,
+        compiler_params=params(),
+        cost_estimate=pl.CostEstimate(
+            flops=6 * 10**9, bytes_accessed=20 * 10**6, transcendentals=10**4
+        ),
+    )(*inputs)
+    inputs = (scalars, low, high, part) + weights
+    rows_halo, part = pl.pallas_call(
+        functools.partial(dense_halo_kernel, atoms),
+        out_shape=[
+            jax.ShapeDtypeStruct((LANES, 10 * LANES), BF16),
+            jax.ShapeDtypeStruct((H, atoms + LANES), BF16),
         ],
+        in_specs=[whole(pltpu.SMEM)] + [whole()] * (len(inputs) - 1),
+        out_specs=[whole()] * 2,
+        scratch_shapes=scratch,
         compiler_params=params(),
     )(*inputs)
     scalar_parts = lax.all_to_all(part.reshape(split, channels, atoms + LANES), "feat", 0, 0)
 
     kinds = shared_scratch(atoms)
     batch = OFFSETS * rows_each
-    names = ["mask", "near", "near_last"] + ["tall"] * 3 + ["many", "stage2"]
+    names = ["mask", "near", "near_last"] + ["tall"] * 3 + ["many", "tall", "row1", "row1"]
     radial, geo = edge_call(
         geometry_kernel,
         atoms,
-        (scalars, rows),
+        (scalars, rows, rows_halo),
         (),
         [],
         [((SPAN, batch, 2 * LANES), BF16), ((SPAN, GEO, batch, LANES), BF16)],
         [kinds[name] for name in names],
     )
-    names = ["weights", "weights", "near", "near_last", "stage4", "loose2"]
-    names += ["loose_low", "pre", "grad_pre", "line", "wide2", "wide2f", "line4", "line1"]
+    names = ["weights", "weights", "near", "near_last", "row2", "loose2"]
+    names += ["pre", "grad_pre", "line", "wide2", "wide2f", "line4", "line1"]
     names += ["low"] * 4 + ["low"] * 4 + ["first"] * 4
     scalar_sum, grads_b, grad_filters_b, pull = edge_call(
         scalar_kernel,
         atoms,
-        (scalars, rows, w_key_filter, w_value_filter[0], scalar_parts),
+        (scalars, rows, rows_halo, w_key_filter, w_value_filter[0], scalar_parts),
         (radial, geo),
         [
             ((R, atoms), BF16),
@@ -1151,14 +1207,14 @@
     share = (EARLY + LATE) // count
     got_vec = lax.all_to_all(send_vec, "feat", 0, 0)
 
-    names = ["weights", "near", "near_last", "stage8", "loose5"]
+    names = ["weights", "near", "near_last", "row4", "loose5"]
     names += ["pre", "grad_pre", "line", "line3"]
     names += ["low"] * 7 + ["low"] * 10 + ["first"] * 10
     rows, _ = lax.optimization_barrier((rows, squares))
     sums, back, grads_a, pos_a, grad_filters_a = edge_call(
         vector_kernel,
         atoms,
-        (scalars, rows, w_value_filter[1], w_value_filter[2]),
+        (scalars, rows, rows_halo, w_value_filter[1], w_value_filter[2]),
         (radial, geo, pull),
         [
             ((3, R, atoms), F32),

time: 201 us -> 200 us (level)
  waiting for transfers between devices: 21.2 us -> 16.5 us
  Pallas kernels: 124 us -> 127 us
    ppermute x1, waiting for transfers between devices: 4.2 us -> 0.01 us  [per_device(): lax.ppermute(ends[1], 'atoms', [(i + 1, i) for i in range(count - 1)])]
    pallas_call x0 -> x1, Pallas kernels: none -> 3.07 us  [per_device(): pl.pallas_call(functools.partial(dense_halo_kernel, atoms), out_shape=[ja...]
  transfers between devices with their start and end apart: 6 -> 6, of which waited for: 4 -> 2; matrix products, arithmetic and copies ran while one was open for 1% -> 1% of each run, Pallas kernels for 32% -> 36%
where the time goes in v1:
time: 200 us; the launch traced here: 199 us
  Pallas kernels  127 us (64%)
  blocking collectives  25.7 us (13%)
  starting transfers between devices  23.9 us (12%)
  waiting for transfers between devices  16.5 us (8%)
  local copies, waits for them, and re-layouts  3.31 us (2%)
  other arithmetic  2.18 us (1%)
    pallas_call x3, Pallas kernels, edge_call(): pl.pallas_call(functools.partial(kernel, molecules, rows, atoms), grid=(S...  96.2 us
    all_to_all x1, blocking collectives, everywhere(): lax.all_to_all(jnp.broadcast_to(x[None], (count,) + x.shape), axis, 0, 0)  16.2 us
    all_gather x1, blocking collectives, per_device(): gathered = lax.all_gather(scalar_sum, 'feat', axis=0, tiled=True)  9.5 us
    all_to_all x1, waiting for transfers between devices, per_device(): got = lax.all_to_all(send, 'feat', 0, 0)  9.38 us
    all_to_all x1, waiting for transfers between devices, per_device(): shares = lax.all_to_all(flat.reshape(count, share, H), 'atoms', 0, 0)  7.12 us
    pallas_call x1, Pallas kernels, per_device(): pl.pallas_call(functools.partial(layer_kernel, atoms), out_shape=[jax.Sha...  7.04 us
    pallas_call x1, Pallas kernels, per_device(): pl.pallas_call(functools.partial(dense_kernel, atoms), out_shape=[jax.Sha...  7 us
    all_to_all x1, starting transfers between devices, per_device(): shares = lax.all_to_all(flat.reshape(count, share, H), 'atoms', 0, 0)  6.96 us
  transfers between devices with their start and end apart: 6, of which 2 were waited for; matrix products, arithmetic and copies ran while one was open for 1% of the time, Pallas kernels for 36%

profile of v1, /device:TPU:0, one launch (start us, length us, event | category | flops | bytes accessed | tf_op | source)
XLA Modules:
  0.0 199.2 jit_solution(17179735376516042665)
XLA Ops:
  0.7 0.6 pad_add_fusion.scalars
  1.2 2.1 %shard_map.272 = (bf16[352,128]{1,0:T(8,128)(2,1)}, bf16[352,128]{1,0:T(8,128)(2,1)}) custom-call(s32[3]{0:T(128)} %pad_add_fusion.scalars, bf16[256,1024]{1,0:T(8,128)(2,1)} %features.7, bf16[3,256,1024]{2,1,0:T(8,128)(2,1)} %vectors.5, bf16[64,1024]{1,0:T(8,128)(2,1)} %cot_f.5, bf16[3,64,1024]{2,1,0:T(8,128)(2,1)} %cot_v.5, s32[32,1024]{1,0:T(8,128)} %refs_11_.1, ...), custom_call_target="tpu_custom_call" | custom-call | tf_op jit(solution)/shard_map/pallas_call | solution.py:725
  3.3 4.8 %collective-permute-start = (bf16[352,128]{1,0:T(8,128)(2,1)}, bf16[352,128]{1,0:T(8,128)(2,1)S(1)}, u32[]{:S(2)}, u32[]{:S(2)}) collective-permute-start(bf16[352,128]{1,0:T(8,128)(2,1)} %get-tuple-element.60), channel_id=1, source_target_pairs={{0,4},{4,8},{8,12},{12,16},{16,20},{20,24},{24,28},{1,5},{5,9},{9,... | collective-permute-start | bytes 270344 | tf_op jit(solution)/shard_map/ppermute | solution.py:1112
  8.2 1.3 collective-permute-start.1
  9.5 0.0 copy-start.7
  9.5 7.0 %shard_map.271 = (bf16[1024,1280]{1,0:T(8,128)(2,1)}, bf16[256,1024]{1,0:T(8,128)(2,1)}, f32[8,1024]{1,0:T(8,128)}) custom-call(s32[3]{0:T(128)} %pad_add_fusion.scalars, bf16[256,1024]{1,0:T(8,128)(2,1)} %features.7, bf16[3,256,1024]{2,1,0:T(8,128)(2,1)} %vectors.5, bf16[64,1024]{1,0:T(8,128)(2,1)} %cot_f.5, bf16[3,64,1024]{2,1,0:T(8,128)(2,1)} %cot_v.5, ...), custom_call_target="tpu_custom_call" | custom-call | flops 6000000000 | bytes 20000000 | tf_op jit(solution)/shard_map/pallas_call | solution.py:1126
  16.5 0.0 copy-done.7
  16.5 0.6 slice_bitcast_fusion
  17.1 0.0 collective-permute-done.low_ref
  17.1 0.0 copy-start.4
  17.1 0.0 collective-permute-done.1.high_ref
  17.1 0.0 copy-start.5
  17.1 0.6 copy-done.4
  17.7 0.0 copy-done.5
  17.8 3.1 %shard_map.273 = (bf16[128,1280]{1,0:T(8,128)(2,1)}, bf16[256,1152]{1,0:T(8,128)(2,1)}) custom-call(s32[3]{0:T(128)} %pad_add_fusion.scalars, bf16[352,128]{1,0:T(8,128)(2,1)} %copy-done.4, bf16[352,128]{1,0:T(8,128)(2,1)} %copy-done.5, bf16[256,1024]{1,0:T(8,128)(2,1)} %get-tuple-element.62.part_in, f32[1,256]{1,0:T(1,128)} %bitcast.50, f32[1,256]{1,0:T(1,128)} %bitcast.55, ...), custom_call_target="tpu_custom_call" | custom-call | tf_op jit(solution)/shard_map/pallas_call | solution.py:1142
  20.8 3.5 %all-to-all-start = ((bf16[4,64,1152]{2,1,0:T(8,128)(2,1)}), bf16[4,64,1152]{2,1,0:T(8,128)(2,1)S(1)}, u32[]{:S(2)}, u32[]{:S(2)}) async-start(bf16[4,64,1152]{2,1,0:T(8,128)(2,1)} %bitcast.28), calls=%async_computation | async-start | bytes 1179648 | tf_op jit(solution)/shard_map/all_to_all | solution.py:1153
  24.3 21.0 %shard_map.274 = (bf16[5,1568,256]{2,1,0:T(8,128)(2,1)}, bf16[5,10,1568,128]{3,2,1,0:T(8,128)(2,1)}) custom-call(s32[3]{0:T(128)} %pad_add_fusion.scalars, bf16[1024,1280]{1,0:T(8,128)(2,1)} %get-tuple-element.75.own_ref, bf16[128,1280]{1,0:T(8,128)(2,1)} %get-tuple-element.63.halo_ref), custom_call_target="tpu_custom_call" | custom-call | flops 20000000000 | bytes 40000000 | tf_op jit(solution)/shard_map/pallas_call | solution.py:634
  45.3 0.0 all-to-all-done.scalar_parts
  45.3 0.0 copy-start.3
  45.3 0.8 copy-done.3
  46.1 34.5 %shard_map.275 = (bf16[64,1024]{1,0:T(8,128)(2,1)}, bf16[192,1024]{1,0:T(8,128)(2,1)}, f32[128,256]{1,0:T(8,128)}, bf16[5,1568,128]{2,1,0:T(8,128)(2,1)}) custom-call(s32[3]{0:T(128)} %pad_add_fusion.scalars, bf16[1024,1280]{1,0:T(8,128)(2,1)} %get-tuple-element.75.own_ref, bf16[128,1280]{1,0:T(8,128)(2,1)} %get-tuple-element.63.halo_ref, ...), custom_call_target="tpu_custom_call" | custom-call | flops 20000000000 | bytes 40000000 | tf_op jit(solution)/shard_map/pallas_call | solution.py:634
  80.6 9.5 %all_gather.3.gathered = bf16[256,1024]{1,0:T(8,128)(2,1)} all-gather(bf16[64,1024]{1,0:T(8,128)(2,1)} %get-tuple-element.67), channel_id=1, replica_groups=mesh['atoms'=8,'feat'=4] {'feat'}, dimensions={0}, use_global_device_ids=true | all-gather | bytes 655360 | tf_op jit(solution)/shard_map/all_gather | solution.py:1183
  90.1 7.0 %shard_map.276 = (bf16[64,1024]{1,0:T(8,128)(2,1)}, f32[3,64,1024]{2,1,0:T(8,128)}, f32[8,1024]{1,0:T(8,128)}, bf16[4,192,1024]{2,1,0:T(8,128)(2,1)}, f32[608,256]{1,0:T(8,128)}) custom-call(s32[3]{0:T(128)} %pad_add_fusion.scalars, bf16[256,1024]{1,0:T(8,128)(2,1)} %features.7, f32[8,1024]{1,0:T(8,128)} %get-tuple-element.58.stat, ...), custom_call_target="tpu_custom_call" | custom-call | tf_op jit(solution)/shard_map/pallas_call | solution.py:1189
  97.2 3.7 %all-to-all-start.1 = ((bf16[4,192,1024]{2,1,0:T(8,128)(2,1)}), bf16[4,192,1024]{2,1,0:T(8,128)(2,1)S(1)}, u32[]{:S(2)}, u32[]{:S(2)}) async-start(bf16[4,192,1024]{2,1,0:T(8,128)(2,1)} %get-tuple-element.72), calls=%async_computation.1 | async-start | bytes 3145728 | tf_op jit(solution)/shard_map/all_to_all | solution.py:1208
  100.9 40.7 %shard_map.277 = (f32[3,64,1024]{2,1,0:T(8,128)}, f32[3,64,1024]{2,1,0:T(8,128)}, bf16[128,1024]{1,0:T(8,128)(2,1)}, f32[8,1024]{1,0:T(8,128)}, f32[128,256]{1,0:T(8,128)}) custom-call(s32[3]{0:T(128)} %pad_add_fusion.scalars, bf16[1024,1280]{1,0:T(8,128)(2,1)} %get-tuple-element.75.own_ref, bf16[128,1280]{1,0:T(8,128)(2,1)} %get-tuple-element.63.halo_ref, ...), custom_call_target="tpu_custom_call" | custom-call | flops 20000000000 | bytes 40000000 | tf_op jit(solution)/shard_map/pallas_call | solution.py:634
  141.6 0.0 all-to-all-done.1.got_vec
  141.6 0.0 copy-start
  141.7 0.0 copy-start.2
  141.7 5.7 %shard_map.278 = (bf16[3,64,1024]{2,1,0:T(8,128)(2,1)}, bf16[4,80,1024]{2,1,0:T(8,128)(2,1)}, bf16[160,256]{1,0:T(8,128)(2,1)}) custom-call(s32[3]{0:T(128)} %pad_add_fusion.scalars, bf16[256,1024]{1,0:T(8,128)(2,1)} %features.7, f32[8,1024]{1,0:T(8,128)} %get-tuple-element.58.stat, bf16[3,256,1024]{2,1,0:T(8,128)(2,1)} %vectors.5, ...), custom_call_target="tpu_custom_call" | custom-call | tf_op jit(solution)/shard_map/pallas_call | solution.py:1235
  147.4 0.0 copy-done
  147.4 0.0 copy-start.6
  147.4 3.6 %all-to-all-start.2 = ((bf16[4,80,1024]{2,1,0:T(8,128)(2,1)}), bf16[4,80,1024]{2,1,0:T(8,128)(2,1)S(1)}, u32[]{:S(2)}, u32[]{:S(2)}) async-start(bf16[4,80,1024]{2,1,0:T(8,128)(2,1)} %get-tuple-element.82), calls=%async_computation.2 | async-start | bytes 1310720 | tf_op jit(solution)/shard_map/all_to_all | solution.py:1247
  151.0 0.0 copy-done.2
  151.1 0.0 copy-done.6
  151.1 0.8 pad_maximum_fusion
  151.9 9.4 %all-to-all-done.2.got = bf16[4,80,1024]{2,1,0:T(8,128)(2,1)S(1)} async-done(((bf16[4,80,1024]{2,1,0:T(8,128)(2,1)}), bf16[4,80,1024]{2,1,0:T(8,128)(2,1)S(1)}, u32[]{:S(2)}, u32[]{:S(2)}) %all-to-all-start.2) | async-done | bytes 655392 | tf_op jit(solution)/shard_map/all_to_all | solution.py:1247
  161.2 0.0 copy-start.1
  161.2 7.0 %all-to-all-start.3 = ((bf16[8,96,256]{2,1,0:T(8,128)(2,1)}), bf16[8,96,256]{2,1,0:T(8,128)(2,1)S(1)}, u32[]{:S(2)}, u32[]{:S(2)}) async-start(bf16[8,96,256]{2,1,0:T(8,128)(2,1)} %bitcast.15), calls=%async_computation.3 | async-start | bytes 786432 | tf_op jit(solution)/shard_map/all_to_all | solution.py:1249
  168.2 0.0 copy-done.1
  168.2 3.7 %shard_map.279 = (f32[64,1024]{1,0:T(8,128)}, f32[3,64,1024]{2,1,0:T(8,128)}, f32[3,1024]{1,0:T(4,128)}, f32[16,256]{1,0:T(8,128)}) custom-call(s32[3]{0:T(128)} %pad_add_fusion.scalars, bf16[4,80,1024]{2,1,0:T(8,128)(2,1)} %copy-done.1, bf16[4,192,1024]{2,1,0:T(8,128)(2,1)} %copy-done, bf16[256,1024]{1,0:T(8,128)(2,1)} %features.7, ...), custom_call_target="tpu_custom_call" | custom-call | tf_op jit(solution)/shard_map/pallas_call | solution.py:1254
  171.9 0.7 convert.7
  172.6 7.1 %all-to-all-done.3 = bf16[8,96,256]{2,1,0:T(8,128)(2,1)S(1)} async-done(((bf16[8,96,256]{2,1,0:T(8,128)(2,1)}), bf16[8,96,256]{2,1,0:T(8,128)(2,1)S(1)}, u32[]{:S(2)}, u32[]{:S(2)}) %all-to-all-start.3) | async-done | bytes 393248 | tf_op jit(solution)/shard_map/all_to_all | solution.py:1249
  179.7 0.1 reduce
  179.9 16.2 %all_to_all.25.got = bf16[8,112,256]{2,1,0:T(8,128)(2,1)} all-to-all(bf16[8,112,256]{2,1,0:T(8,128)(2,1)S(1)} %broadcast_in_dim.2), channel_id=1, replica_groups=mesh['atoms'=8,'feat'=4] {'atoms'}, dimensions={0} | all-to-all | bytes 917504 | tf_op jit(solution)/shard_map/all_to_all | solution.py:1085
  196.1 2.0 %shard_map.280 = (f32[1,64]{1,0:T(1,128)}, f32[1,64]{1,0:T(1,128)}, f32[64,256]{1,0:T(8,128)}, f32[64,256]{1,0:T(8,128)}, f32[3,64,256]{2,1,0:T(8,128)}, /*index...) custom-call(bf16[8,112,256]{2,1,0:T(8,128)(2,1)} %all_to_all.25.got), custom_call_target="tpu_custom_call" | custom-call | tf_op jit(solution)/shard_map/pallas_call | solution.py:1271
  198.1 1.2 slice_bitcast_fusion.3
  (3 shorter events, 0.1 us)
Async XLA Ops:
  3.3 13.8 %collective-permute-start = (bf16[352,128]{1,0:T(8,128)(2,1)}, bf16[352,128]{1,0:T(8,128)(2,1)S(1)}, u32[]{:S(2)}, u32[]{:S(2)}) collective-permute-start(bf16[352,128]{1,0:T(8,128)(2,1)} %get-tuple-element.60), channel_id=1, source_target_pairs={{0,4},{4,8},{8,12},{12,16},{16,20},{20,24},{24,28},{1,5},{5,9},{9,... | collective-permute-start | bytes 270344 | tf_op jit(solution)/shard_map/ppermute | solution.py:1112
  8.2 8.9 %collective-permute-start.1 = (bf16[352,128]{1,0:T(8,128)(2,1)}, bf16[352,128]{1,0:T(8,128)(2,1)S(1)}, u32[]{:S(2)}, u32[]{:S(2)}) collective-permute-start(bf16[352,128]{1,0:T(8,128)(2,1)} %get-tuple-element.61), channel_id=1, source_target_pairs={{4,0},{8,4},{12,8},{16,12},{20,16},{24,20},{28,24},{5,1},{9,5},{13... | collective-permute-start | bytes 270344 | tf_op jit(solution)/shard_map/ppermute | solution.py:1113
  9.5 7.0 %copy-start.7 = (bf16[3,64,64]{2,1,0:T(8,128)(2,1)S(1)}, bf16[3,64,64]{2,1,0:T(8,128)(2,1)}, u32[]{:S(2)}) copy-start(bf16[3,64,64]{2,1,0:T(8,128)(2,1)} %param.29) | copy-start | bytes 73732
  17.1 0.6 copy-start.4
  17.1 0.7 copy-start.5
  20.8 24.5 %all-to-all-start = ((bf16[4,64,1152]{2,1,0:T(8,128)(2,1)}), bf16[4,64,1152]{2,1,0:T(8,128)(2,1)S(1)}, u32[]{:S(2)}, u32[]{:S(2)}) async-start(bf16[4,64,1152]{2,1,0:T(8,128)(2,1)} %bitcast.28), calls=%async_computation | async-start | bytes 1179648 | tf_op jit(solution)/shard_map/all_to_all | solution.py:1153
  45.3 0.8 copy-start.3
  97.2 44.5 %all-to-all-start.1 = ((bf16[4,192,1024]{2,1,0:T(8,128)(2,1)}), bf16[4,192,1024]{2,1,0:T(8,128)(2,1)S(1)}, u32[]{:S(2)}, u32[]{:S(2)}) async-start(bf16[4,192,1024]{2,1,0:T(8,128)(2,1)} %get-tuple-element.72), calls=%async_computation.1 | async-start | bytes 3145728 | tf_op jit(solution)/shard_map/all_to_all | solution.py:1208
  141.6 5.7 %copy-start = (bf16[4,192,1024]{2,1,0:T(8,128)(2,1)}, bf16[4,192,1024]{2,1,0:T(8,128)(2,1)S(1)}, u32[]{:S(2)}) copy-start(bf16[4,192,1024]{2,1,0:T(8,128)(2,1)S(1)} %all-to-all-done.1.got_vec) | copy-start | bytes 4718596
  141.7 9.4 %copy-start.2 = (f32[608,256]{1,0:T(8,128)S(1)}, f32[608,256]{1,0:T(8,128)}, u32[]{:S(2)}) copy-start(f32[608,256]{1,0:T(8,128)} %get-tuple-element.88) | copy-start | bytes 1867780
  147.4 3.7 %copy-start.6 = (bf16[160,256]{1,0:T(8,128)(2,1)S(1)}, bf16[160,256]{1,0:T(8,128)(2,1)}, u32[]{:S(2)}) copy-start(bf16[160,256]{1,0:T(8,128)(2,1)} %get-tuple-element.89) | copy-start | bytes 245764
  147.4 13.8 %all-to-all-start.2 = ((bf16[4,80,1024]{2,1,0:T(8,128)(2,1)}), bf16[4,80,1024]{2,1,0:T(8,128)(2,1)S(1)}, u32[]{:S(2)}, u32[]{:S(2)}) async-start(bf16[4,80,1024]{2,1,0:T(8,128)(2,1)} %get-tuple-element.82), calls=%async_computation.2 | async-start | bytes 1310720 | tf_op jit(solution)/shard_map/all_to_all | solution.py:1247
  161.2 7.0 %copy-start.1 = (bf16[4,80,1024]{2,1,0:T(8,128)(2,1)}, bf16[4,80,1024]{2,1,0:T(8,128)(2,1)S(1)}, u32[]{:S(2)}) copy-start(bf16[4,80,1024]{2,1,0:T(8,128)(2,1)S(1)} %all-to-all-done.2.got) | copy-start | bytes 1966084
  161.2 18.5 %all-to-all-start.3 = ((bf16[8,96,256]{2,1,0:T(8,128)(2,1)}), bf16[8,96,256]{2,1,0:T(8,128)(2,1)S(1)}, u32[]{:S(2)}, u32[]{:S(2)}) async-start(bf16[8,96,256]{2,1,0:T(8,128)(2,1)} %bitcast.15), calls=%async_computation.3 | async-start | bytes 786432 | tf_op jit(solution)/shard_map/all_to_all | solution.py:1249

commit v2 on v1

--- a/solution.py
+++ b/solution.py
@@ -133,14 +133,23 @@
     return place
 
 
-def assemble(target, own_ref, halo_ref, lanes, at=0):
-    atoms, tall, size = own_ref.shape[0], target.shape[0], lanes.stop - lanes.start
-    there = slice(at, at + size)
-    target[HALO : HALO + atoms, there] = own_ref[:, lanes]
-    target[:HALO, there] = halo_ref[:HALO, lanes]
+def assemble(target, own_ref, halo_ref, lanes, shift=0):
+    atoms, tall = own_ref.shape[0], target.shape[0]
+    also = slice(lanes.start + shift, lanes.stop + shift)
+    target[HALO : HALO + atoms] = own_ref[:, lanes]
+    target[:HALO] = halo_ref[:HALO, also]
     end = 2 * HALO + atoms
-    target[HALO + atoms : end, there] = halo_ref[HALO : 2 * HALO, lanes]
-    target[end:, there] = jnp.zeros((tall - end, size), BF16)
+    target[HALO + atoms : end] = halo_ref[HALO : 2 * HALO, also]
+    target[end:] = jnp.zeros((tall - end, target.shape[1]), BF16)
+
+
+def keep_own(radial, owned, target, rows):
+    def step(k, _):
+        here = pl.ds(pl.multiple_of(k * rows, SUB), rows)
+        target[here, :] = radial[here, :LANES] * owned[...].astype(BF16)
+        return 0
+
+    lax.fori_loop(0, OFFSETS, step, 0)
 
 
 def collect(sources, target, blocks, distances, start):
@@ -213,11 +222,12 @@
 
 COSINE = (0.9999999998, -0.04934802137, 0.000405870916, -1.335212003e-06, 2.349373138e-09, -2.43963243e-12)
 
-GEO_ENVELOPE, GEO_BEND, GEO_INVERSE, GEO_INTO, GEO_FROM, GEO_WAY, GEO_SLOPE, GEO_OWN = 0, 1, 2, 3, 4, 5, 8, 9
-GEO = 10
-
-
-def geometry(pos, many, t, rows, owned, radial, geo):
+GEO_SLOPE, GEO_INTO, GEO_FROM = 0, 1, 2
+GEO_ENVELOPE, GEO_BEND = 0, 1
+GEO_INVERSE, GEO_WAY = 0, 1
+
+
+def geometry(pos, many, t, rows, radial, geo, geo_s, geo_v):
     inv_space = (R - 1) / CUTOFF
 
     def step(k, _):
@@ -225,7 +235,6 @@
             here = pl.ds(pl.multiple_of(k * rows + o, SUB), size)
             part = slice(o, o + size)
             off = [p[t, part] - p[t + 1 + k, part] for p in pos]
-            mine = owned[part].astype(BF16)
             close = many[t, part]
             lane = lax.broadcasted_iota(jnp.int32, (size, LANES), 1)
             base = jnp.where(lane >= R, R, 0)
@@ -248,14 +257,13 @@
             slope = bump * bend - inv_space * (u * value)
             radial[here, :LANES] = high
             radial[here, LANES:] = (value - high.astype(F32)).astype(BF16)
-            geo[GEO_OWN, here, :] = high * mine
             geo[GEO_SLOPE, here, :] = slope.astype(BF16)
-            geo[GEO_BEND, here, :] = bend.astype(BF16)
-            geo[GEO_ENVELOPE, here, :] = envelope.astype(BF16)
+            geo_s[GEO_BEND, here, :] = bend.astype(BF16)
+            geo_s[GEO_ENVELOPE, here, :] = envelope.astype(BF16)
             for d in range(3):
-                geo[GEO_WAY + d, here, :] = (off[d] * inverse).astype(BF16)
+                geo_v[GEO_WAY + d, here, :] = (off[d] * inverse).astype(BF16)
             signed = jnp.where(square > 0.01, inverse, -inverse)
-            geo[GEO_INVERSE, here, :] = signed.astype(BF16)
+            geo_v[GEO_INVERSE, here, :] = signed.astype(BF16)
             into = jnp.take_along_axis(close, near, axis=1)
             out_of = jnp.take_along_axis(close, near + 32, axis=1)
             geo[GEO_INTO, here, :] = into.astype(BF16)
@@ -320,8 +328,8 @@
 
 def geometry_kernel(
     molecules, rows, atoms,
-    scalars, own_ref, halo_ref, radial_out, geo_out,
-    owned, near, near_last, px, py, pz, many, count, all_pos, all_count,
+    scalars, own_count, own_pos, halo_ref, radial_out, geo_out, geo_s_out, geo_v_out,
+    near, near_last, px, py, pz, many, count, all_pos, all_count,
 ):
     t = pl.program_id(0)
     start = scalars[0]
@@ -330,24 +338,24 @@
 
     @pl.when(t == 0)
     def _():
-        row_masks(owned, start, blocks, atoms)
         set_distances(near, blocks[0][1], blocks[0][2])
         set_distances(near_last, blocks[-1][1], blocks[-1][2])
-        assemble(all_pos, own_ref, halo_ref, slice(POS * LANES, (POS + 1) * LANES))
-        assemble(all_count, own_ref, halo_ref, slice(C2_COUNT * LANES, (C2_COUNT + 1) * LANES))
+        assemble(all_pos, own_pos, halo_ref, slice(0, LANES), POS * LANES)
+        assemble(all_count, own_count, halo_ref, slice(0, LANES), C2_COUNT * LANES)
         extra = position_spreader(all_pos, (px, py, pz))
         spread(all_count, (None, count), blocks, distances, start, extra)
         set_multiplicities(count, many, blocks, rows)
 
-    geometry((px, py, pz), many, t, rows, owned, radial_out.at[0], geo_out.at[0])
+    outs = [ref.at[0] for ref in (radial_out, geo_out, geo_s_out, geo_v_out)]
+    geometry((px, py, pz), many, t, rows, *outs)
 
 
 def vector_kernel(
     molecules, rows, atoms,
-    scalars, own_ref, halo_ref, filter_1, filter_2, radial_in, geo_in, pull_in,
+    scalars, own_ref, halo_ref, filter_1, filter_2, radial_in, geo_in, geo_v_in, pull_in,
     sums_ref, back_ref, grads_ref, pos_out, grad_w_ref,
     weights_ref, near, near_last, all_rows, loose, pre, grad_pre,
-    grad_radial, grad_ways,
+    grad_radial, grad_ways, owned, radial_own,
     w0, w1, w2, v2, c0, c1, c2,
     s0, s1, s2, a0, a1, a2, gv, gx, gy, gz,
     fs0, fs1, fs2, fa0, fa1, fa2, fgv, fgx, fgy, fgz,
@@ -355,7 +363,7 @@
     t = pl.program_id(0)
     start = scalars[0]
     own = slice(HALO, HALO + atoms)
-    radial, geo = radial_in.at[0], geo_in.at[0]
+    radial, geo, geo_v = radial_in.at[0], geo_in.at[0], geo_v_in.at[0]
     w, c, g_pos = (w0, w1, w2), (c0, c1, c2), (gx, gy, gz)
     sums, backs = (s0, s1, s2), (a0, a1, a2)
     blocks = block_list(molecules, rows)
@@ -364,6 +372,7 @@
     @pl.when(t == 0)
     def _():
         set_filters(weights_ref, filter_1, filter_2)
+        row_masks(owned, start, blocks, atoms)
         set_distances(near, blocks[0][1], blocks[0][2])
         set_distances(near_last, blocks[-1][1], blocks[-1][2])
         assemble(all_rows, own_ref, halo_ref, slice(W01 * LANES, (C2_COUNT + 1) * LANES))
@@ -373,12 +382,13 @@
         grad_w_ref[...] = jnp.zeros(grad_w_ref.shape, F32)
 
     pre[...] = dot(radial[...], weights_ref[...])
+    keep_own(radial, owned, radial_own, rows)
 
     def channel(o, here, ii, jj, k):
         h1, h2 = pre[here, :LANES], pre[here, LANES:]
         ni, nj = geo[GEO_INTO, here, :], geo[GEO_FROM, here, :]
         v2i, v2j = v2[ii], v2[jj]
-        ways = [geo[GEO_WAY + d, here, :] for d in range(3)]
+        ways = [geo_v[GEO_WAY + d, here, :] for d in range(3)]
         wi, wj = [w[d][ii] for d in range(3)], [w[d][jj] for d in range(3)]
         ci, cj = [c[d][ii] for d in range(3)], [c[d][jj] for d in range(3)]
         old_sums = [sums[d][jj] for d in range(3)]
@@ -417,13 +427,13 @@
 
     carried(rows, t, (fs0, fs1, fs2, fa0, fa1, fa2, fgv), 2, channel)
     grad_radial[...] = dot_nt(grad_pre[...], weights_ref[:LANES])
-    grad_w_ref[...] = grad_w_ref[...] + dot_tn(geo[GEO_OWN], grad_pre[...])
+    grad_w_ref[...] = grad_w_ref[...] + dot_tn(radial_own[...], grad_pre[...])
 
     def turn(o, here, ii, jj, k):
-        ways = [geo[GEO_WAY + d, here, :] for d in range(3)]
+        ways = [geo_v[GEO_WAY + d, here, :] for d in range(3)]
         grads = [grad_ways[d, here, :] for d in range(3)]
         grad, slope = grad_radial[here, :], geo[GEO_SLOPE, here, :]
-        signed, more = geo[GEO_INVERSE, here, :], pull_in[0, here, :]
+        signed, more = geo_v[GEO_INVERSE, here, :], pull_in[0, here, :]
         old = [g[jj] for g in g_pos]
 
         def compute():
@@ -475,10 +485,10 @@
 
 def scalar_kernel(
     molecules, rows, atoms,
-    scalars, own_ref, halo_ref, filter_1, filter_2, scalar_parts, radial_in, geo_in,
+    scalars, own_ref, halo_ref, filter_1, filter_2, scalar_parts, radial_in, geo_in, geo_s_in,
     sum_ref, grads_ref, grad_w_ref, pull_out,
     weights_ref, heads_ref, near, near_last, all_rows, loose, pre,
-    grad_pre, grad_radial, products, sums, gates, bends,
+    grad_pre, grad_radial, products, sums, gates, bends, owned, radial_own,
     q, key, v0, gs,
     ss, gq, gk, g0,
     fss, fgq, fgk, fg0,
@@ -486,7 +496,7 @@
     t = pl.program_id(0)
     start = scalars[0]
     own = slice(HALO, HALO + atoms)
-    radial, geo = radial_in.at[0], geo_in.at[0]
+    radial, geo, geo_s = radial_in.at[0], geo_in.at[0], geo_s_in.at[0]
     blocks = block_list(molecules, rows)
     distances = (near, near_last)
 
@@ -496,6 +506,7 @@
         row = lax.broadcasted_iota(jnp.int32, (2 * LANES, 2 * LANES), 0)
         lane = lax.broadcasted_iota(jnp.int32, (2 * LANES, 2 * LANES), 1)
         heads_ref[...] = jnp.where(row // HEAD == lane // HEAD, 1.0, 0.0).astype(BF16)
+        row_masks(owned, start, blocks, atoms)
         set_distances(near, blocks[0][1], blocks[0][2])
         set_distances(near_last, blocks[-1][1], blocks[-1][2])
         assemble(all_rows, own_ref, halo_ref, slice(QK * LANES, (V0 + 1) * LANES))
@@ -517,6 +528,7 @@
         grad_w_ref[...] = jnp.zeros(grad_w_ref.shape, F32)
 
     pre[...] = dot(radial[...], weights_ref[...])
+    keep_own(radial, owned, radial_own, rows)
 
     def multiply(k, _):
         for o, size in halves(rows):
@@ -542,7 +554,7 @@
 
     def channel(o, here, ii, jj, k):
         fk, f0, dk, d0 = [gates[n, here, :] for n in range(4)]
-        envelope, bend = geo[GEO_ENVELOPE, here, :], geo[GEO_BEND, here, :]
+        envelope, bend = geo_s[GEO_ENVELOPE, here, :], geo_s[GEO_BEND, here, :]
         side_in = []
         for side in range(2):
             lanes = slice(side * LANES, (side + 1) * LANES)
@@ -581,7 +593,7 @@
 
     carried(rows, t, (fss, fgq, fg0, fgk), 2, channel)
     grad_radial[...] = dot_nt(grad_pre[...], weights_ref[:LANES])
-    grad_w_ref[...] = grad_w_ref[...] + dot_tn(geo[GEO_OWN], grad_pre[...])
+    grad_w_ref[...] = grad_w_ref[...] + dot_tn(radial_own[...], grad_pre[...])
 
     def pull(k, _):
         here = pl.ds(pl.multiple_of(k * rows, SUB), rows)
@@ -629,14 +641,15 @@
     return pl.BlockSpec(shape, lambda t: zeros)
 
 
-def edge_call(kernel, atoms, inputs, stepped_in, outs, stepped_out, scratch):
+def edge_call(kernel, atoms, inputs, stepped_in, outs, stepped_out, scratch, columns=()):
     molecules, rows, _ = edge_sizes(atoms)
     return pl.pallas_call(
         functools.partial(kernel, molecules, rows, atoms),
         grid=(SPAN,),
         out_shape=[jax.ShapeDtypeStruct(s, kind) for s, kind in outs + stepped_out],
         in_specs=[whole(pltpu.SMEM)]
-        + [fixed(x.shape) for x in inputs[1:]]
+        + [pl.BlockSpec((atoms, LANES), lambda t, n=n: (0, n)) for n in columns]
+        + [fixed(x.shape) for x in inputs[1 + len(columns) :]]
         + [by_step(x.shape) for x in stepped_in],
         out_specs=[fixed(s) for s, _ in outs] + [by_step(s) for s, _ in stepped_out],
         scratch_shapes=[pltpu.VMEM(s, kind) for s, kind in scratch],
@@ -1049,7 +1062,7 @@
     numbers = total[:, LANES : LANES + 1]
     size = jnp.where(lax.broadcasted_iota(jnp.int32, (8, 1), 0) < 2, 1.0, 3.0) * H
     rms = jnp.sqrt(numbers / (numbers[4:5] * size) + 1e-06)
-    rms_ref[...] = jnp.broadcast_to(rms, (8, LANES)).T[:1, :8]
+    rms_ref[...] = jnp.broadcast_to(rms, (8, LANES)).T[:1, :4]
     order = [(g, p) for g in (g_vector, g_output) for p in range(3)]
     order += [(g_query, None), (g_key, None), (g_value, 0), ((g_key_f, None), (g_value_f, 0))]
     order += [(g_value, 1), (g_value, 2), ((g_value_f, 1), (g_value_f, 2))]
@@ -1154,24 +1167,27 @@
 
     kinds = shared_scratch(atoms)
     batch = OFFSETS * rows_each
-    names = ["mask", "near", "near_last"] + ["tall"] * 3 + ["many", "tall", "row1", "row1"]
-    radial, geo = edge_call(
+    names = ["near", "near_last"] + ["tall"] * 3 + ["many", "tall", "row1", "row1"]
+    radial, geo, geo_s, geo_v = edge_call(
         geometry_kernel,
         atoms,
-        (scalars, rows, rows_halo),
+        (scalars, rows, rows, rows_halo),
         (),
         [],
-        [((SPAN, batch, 2 * LANES), BF16), ((SPAN, GEO, batch, LANES), BF16)],
+        [((SPAN, batch, 2 * LANES), BF16)]
+        + [((SPAN, n, batch, LANES), BF16) for n in (3, 2, 4)],
         [kinds[name] for name in names],
+        (C2_COUNT, POS),
     )
     names = ["weights", "weights", "near", "near_last", "row2", "loose2"]
     names += ["pre", "grad_pre", "line", "wide2", "wide2f", "line4", "line1"]
+    names += ["mask", "line1"]
     names += ["low"] * 4 + ["low"] * 4 + ["first"] * 4
     scalar_sum, grads_b, grad_filters_b, pull = edge_call(
         scalar_kernel,
         atoms,
         (scalars, rows, rows_halo, w_key_filter, w_value_filter[0], scalar_parts),
-        (radial, geo),
+        (radial, geo, geo_s),
         [
             ((R, atoms), BF16),
             ((3 * R, atoms), BF16),
@@ -1208,14 +1224,14 @@
     got_vec = lax.all_to_all(send_vec, "feat", 0, 0)
 
     names = ["weights", "near", "near_last", "row4", "loose5"]
-    names += ["pre", "grad_pre", "line", "line3"]
+    names += ["pre", "grad_pre", "line", "line3", "mask", "line1"]
     names += ["low"] * 7 + ["low"] * 10 + ["first"] * 10
     rows, _ = lax.optimization_barrier((rows, squares))
     sums, back, grads_a, pos_a, grad_filters_a = edge_call(
         vector_kernel,
         atoms,
         (scalars, rows, rows_halo, w_value_filter[1], w_value_filter[2]),
-        (radial, geo, pull),
+        (radial, geo, geo_v, pull),
         [
             ((3, R, atoms), F32),
             ((3, R, atoms), F32),
@@ -1266,7 +1282,7 @@
     mine = jnp.concatenate([jnp.sum(shares.astype(F32), axis=0), small], axis=0).astype(BF16)
     every = everywhere(mine, "atoms")
     shapes = [
-        (1, R), (1, R), (R, H), (R, H), (3, R, H), (3, R, H), (3, R, H), (R, R), (3, R, R), (1, 8),
+        (1, R), (1, R), (R, H), (R, H), (3, R, H), (3, R, H), (3, R, H), (R, R), (3, R, R), (1, 4),
     ]
     grads = pl.pallas_call(
         functools.partial(unpack_kernel, share),
@@ -1290,7 +1306,7 @@
         jnp.swapaxes(grads[6], 1, 2),
         grads[7],
         grads[8],
-        grads[9][0, :4],
+        grads[9].reshape(4),
     )
 
 

time: 200 us -> 198 us (0.990)
  transfers between devices with their start and end apart: 6 -> 6, of which waited for: 2 -> 2; matrix products, arithmetic and copies ran while one was open for 1% -> 2% of each run, Pallas kernels for 36% -> 36%
where the time goes in v2:
time: 198 us; the launch traced here: 197 us
  Pallas kernels  126 us (64%)
  blocking collectives  25.7 us (13%)
  starting transfers between devices  23.8 us (12%)
  waiting for transfers between devices  15.6 us (8%)
  other arithmetic  3.07 us (2%)
  local copies, waits for them, and re-layouts  2.13 us (1%)
    pallas_call x3, Pallas kernels, edge_call(): pl.pallas_call(functools.partial(kernel, molecules, rows, atoms), grid=(S...  95.4 us
    all_to_all x1, blocking collectives, everywhere(): lax.all_to_all(jnp.broadcast_to(x[None], (count,) + x.shape), axis, 0, 0)  16.2 us
    all_gather x1, blocking collectives, per_device(): gathered = lax.all_gather(scalar_sum, 'feat', axis=0, tiled=True)  9.48 us
    all_to_all x1, waiting for transfers between devices, per_device(): got = lax.all_to_all(send, 'feat', 0, 0)  8.5 us
    all_to_all x1, waiting for transfers between devices, per_device(): shares = lax.all_to_all(flat.reshape(count, share, H), 'atoms', 0, 0)  7.12 us
    pallas_call x1, Pallas kernels, per_device(): pl.pallas_call(functools.partial(layer_kernel, atoms), out_shape=[jax.Sha...  7.06 us
    pallas_call x1, Pallas kernels, per_device(): pl.pallas_call(functools.partial(dense_kernel, atoms), out_shape=[jax.Sha...  7.04 us
    all_to_all x1, starting transfers between devices, per_device(): shares = lax.all_to_all(flat.reshape(count, share, H), 'atoms', 0, 0)  6.97 us
  transfers between devices with their start and end apart: 6, of which 2 were waited for; matrix products, arithmetic and copies ran while one was open for 2% of the time, Pallas kernels for 36%

profile of v2, /device:TPU:0, one launch (start us, length us, event | category | flops | bytes accessed | tf_op | source)
XLA Modules:
  0.0 197.2 jit_solution(7539248087623057762)
XLA Ops:
  0.7 0.6 pad_add_fusion.scalars
  1.2 2.1 %shard_map.272 = (bf16[352,128]{1,0:T(8,128)(2,1)}, bf16[352,128]{1,0:T(8,128)(2,1)}) custom-call(s32[3]{0:T(128)} %pad_add_fusion.scalars, bf16[256,1024]{1,0:T(8,128)(2,1)} %features.7, bf16[3,256,1024]{2,1,0:T(8,128)(2,1)} %vectors.5, bf16[64,1024]{1,0:T(8,128)(2,1)} %cot_f.5, bf16[3,64,1024]{2,1,0:T(8,128)(2,1)} %cot_v.5, s32[32,1024]{1,0:T(8,128)} %refs_11_.1, ...), custom_call_target="tpu_custom_call" | custom-call | tf_op jit(solution)/shard_map/pallas_call | solution.py:738
  3.3 4.8 %collective-permute-start = (bf16[352,128]{1,0:T(8,128)(2,1)}, bf16[352,128]{1,0:T(8,128)(2,1)S(1)}, u32[]{:S(2)}, u32[]{:S(2)}) collective-permute-start(bf16[352,128]{1,0:T(8,128)(2,1)} %get-tuple-element.62), channel_id=1, source_target_pairs={{0,4},{4,8},{8,12},{12,16},{16,20},{20,24},{24,28},{1,5},{5,9},{9,... | collective-permute-start | bytes 270344 | tf_op jit(solution)/shard_map/ppermute | solution.py:1125
  8.2 1.3 collective-permute-start.1
  9.5 0.0 copy-start.6
  9.5 7.0 %shard_map.271 = (bf16[1024,1280]{1,0:T(8,128)(2,1)}, bf16[256,1024]{1,0:T(8,128)(2,1)}, f32[8,1024]{1,0:T(8,128)}) custom-call(s32[3]{0:T(128)} %pad_add_fusion.scalars, bf16[256,1024]{1,0:T(8,128)(2,1)} %features.7, bf16[3,256,1024]{2,1,0:T(8,128)(2,1)} %vectors.5, bf16[64,1024]{1,0:T(8,128)(2,1)} %cot_f.5, bf16[3,64,1024]{2,1,0:T(8,128)(2,1)} %cot_v.5, ...), custom_call_target="tpu_custom_call" | custom-call | flops 6000000000 | bytes 20000000 | tf_op jit(solution)/shard_map/pallas_call | solution.py:1139
  16.5 0.0 copy-done.6
  16.5 0.6 slice_bitcast_fusion
  17.1 0.0 collective-permute-done.low_ref
  17.1 0.0 copy-start.4
  17.1 0.0 collective-permute-done.1.high_ref
  17.1 0.0 copy-start.5
  17.2 0.6 copy-done.4
  17.8 0.0 copy-done.5
  17.8 3.1 %shard_map.273 = (bf16[128,1280]{1,0:T(8,128)(2,1)}, bf16[256,1152]{1,0:T(8,128)(2,1)}) custom-call(s32[3]{0:T(128)} %pad_add_fusion.scalars, bf16[352,128]{1,0:T(8,128)(2,1)} %copy-done.4, bf16[352,128]{1,0:T(8,128)(2,1)} %copy-done.5, bf16[256,1024]{1,0:T(8,128)(2,1)} %get-tuple-element.64.part_in, f32[1,256]{1,0:T(1,128)} %bitcast.49, f32[1,256]{1,0:T(1,128)} %bitcast.54, ...), custom_call_target="tpu_custom_call" | custom-call | tf_op jit(solution)/shard_map/pallas_call | solution.py:1155
  20.9 3.5 %all-to-all-start = ((bf16[4,64,1152]{2,1,0:T(8,128)(2,1)}), bf16[4,64,1152]{2,1,0:T(8,128)(2,1)S(1)}, u32[]{:S(2)}, u32[]{:S(2)}) async-start(bf16[4,64,1152]{2,1,0:T(8,128)(2,1)} %bitcast.27), calls=%async_computation | async-start | bytes 1179648 | tf_op jit(solution)/shard_map/all_to_all | solution.py:1166
  24.4 20.4 %shard_map.274 = (bf16[5,1568,256]{2,1,0:T(8,128)(2,1)}, bf16[5,3,1568,128]{3,2,1,0:T(8,128)(2,1)}, bf16[5,2,1568,128]{3,2,1,0:T(8,128)(2,1)}, bf16[5,4,1568,128]{3,2,1,0:T(8,128)(2,1)}) custom-call(s32[3]{0:T(128)} %pad_add_fusion.scalars, bf16[1024,1280]{1,0:T(8,128)(2,1)} %get-tuple-element.78.own_count.own_pos.own_ref, ...), custom_call_target="tpu_custom_call" | custom-call | flops 20000000000 | bytes 40000000 | tf_op jit(solution)/shard_map/pallas_call | solution.py:646
  44.8 0.0 all-to-all-done.scalar_parts
  44.8 0.0 copy-start.3
  44.8 0.8 copy-done.3
  45.6 34.7 %shard_map.275 = (bf16[64,1024]{1,0:T(8,128)(2,1)}, bf16[192,1024]{1,0:T(8,128)(2,1)}, f32[128,256]{1,0:T(8,128)}, bf16[5,1568,128]{2,1,0:T(8,128)(2,1)}) custom-call(s32[3]{0:T(128)} %pad_add_fusion.scalars, bf16[1024,1280]{1,0:T(8,128)(2,1)} %get-tuple-element.78.own_count.own_pos.own_ref, bf16[128,1280]{1,0:T(8,128)(2,1)} %get-tuple-element.65.halo_ref, ...), custom_call_target="tpu_custom_call" | custom-call | flops 20000000000 | bytes 40000000 | tf_op jit(solution)/shard_map/pallas_call | solution.py:646
  80.3 9.5 %all_gather.3.gathered = bf16[256,1024]{1,0:T(8,128)(2,1)} all-gather(bf16[64,1024]{1,0:T(8,128)(2,1)} %get-tuple-element.70), channel_id=1, replica_groups=mesh['atoms'=8,'feat'=4] {'feat'}, dimensions={0}, use_global_device_ids=true | all-gather | bytes 655360 | tf_op jit(solution)/shard_map/all_gather | solution.py:1199
  89.8 7.1 %shard_map.276 = (bf16[64,1024]{1,0:T(8,128)(2,1)}, f32[3,64,1024]{2,1,0:T(8,128)}, f32[8,1024]{1,0:T(8,128)}, bf16[4,192,1024]{2,1,0:T(8,128)(2,1)}, f32[608,256]{1,0:T(8,128)}) custom-call(s32[3]{0:T(128)} %pad_add_fusion.scalars, bf16[256,1024]{1,0:T(8,128)(2,1)} %features.7, f32[8,1024]{1,0:T(8,128)} %get-tuple-element.60.stat, ...), custom_call_target="tpu_custom_call" | custom-call | tf_op jit(solution)/shard_map/pallas_call | solution.py:1205
  96.8 3.7 %all-to-all-start.1 = ((bf16[4,192,1024]{2,1,0:T(8,128)(2,1)}), bf16[4,192,1024]{2,1,0:T(8,128)(2,1)S(1)}, u32[]{:S(2)}, u32[]{:S(2)}) async-start(bf16[4,192,1024]{2,1,0:T(8,128)(2,1)} %get-tuple-element.75), calls=%async_computation.1 | async-start | bytes 3145728 | tf_op jit(solution)/shard_map/all_to_all | solution.py:1224
  100.6 40.3 %shard_map.277 = (f32[3,64,1024]{2,1,0:T(8,128)}, f32[3,64,1024]{2,1,0:T(8,128)}, bf16[128,1024]{1,0:T(8,128)(2,1)}, f32[8,1024]{1,0:T(8,128)}, f32[128,256]{1,0:T(8,128)}) custom-call(s32[3]{0:T(128)} %pad_add_fusion.scalars, bf16[1024,1280]{1,0:T(8,128)(2,1)} %get-tuple-element.78.own_count.own_pos.own_ref, bf16[128,1280]{1,0:T(8,128)(2,1)} %get-tuple-element.65.halo_ref, ...), custom_call_target="tpu_custom_call" | custom-call | flops 20000000000 | bytes 40000000 | tf_op jit(solution)/shard_map/pallas_call | solution.py:646
  140.9 0.0 all-to-all-done.1.got_vec
  140.9 0.0 copy-start
  140.9 0.0 copy-start.2
  140.9 5.7 %shard_map.278 = (bf16[3,64,1024]{2,1,0:T(8,128)(2,1)}, bf16[4,80,1024]{2,1,0:T(8,128)(2,1)}, bf16[160,256]{1,0:T(8,128)(2,1)}) custom-call(s32[3]{0:T(128)} %pad_add_fusion.scalars, bf16[256,1024]{1,0:T(8,128)(2,1)} %features.7, f32[8,1024]{1,0:T(8,128)} %get-tuple-element.60.stat, bf16[3,256,1024]{2,1,0:T(8,128)(2,1)} %vectors.5, ...), custom_call_target="tpu_custom_call" | custom-call | tf_op jit(solution)/shard_map/pallas_call | solution.py:1251
  146.6 0.0 copy-done
  146.6 3.5 %all-to-all-start.2 = ((bf16[4,80,1024]{2,1,0:T(8,128)(2,1)}), bf16[4,80,1024]{2,1,0:T(8,128)(2,1)S(1)}, u32[]{:S(2)}, u32[]{:S(2)}) async-start(bf16[4,80,1024]{2,1,0:T(8,128)(2,1)} %get-tuple-element.86), calls=%async_computation.2 | async-start | bytes 1310720 | tf_op jit(solution)/shard_map/all_to_all | solution.py:1263
  150.1 0.0 copy-done.2
  150.2 1.7 pad_maximum_fusion
  151.8 8.5 %all-to-all-done.2.got = bf16[4,80,1024]{2,1,0:T(8,128)(2,1)S(1)} async-done(((bf16[4,80,1024]{2,1,0:T(8,128)(2,1)}), bf16[4,80,1024]{2,1,0:T(8,128)(2,1)S(1)}, u32[]{:S(2)}, u32[]{:S(2)}) %all-to-all-start.2) | async-done | bytes 655392 | tf_op jit(solution)/shard_map/all_to_all | solution.py:1263
  160.3 0.0 copy-start.1
  160.3 7.0 %all-to-all-start.3 = ((bf16[8,96,256]{2,1,0:T(8,128)(2,1)}), bf16[8,96,256]{2,1,0:T(8,128)(2,1)S(1)}, u32[]{:S(2)}, u32[]{:S(2)}) async-start(bf16[8,96,256]{2,1,0:T(8,128)(2,1)} %bitcast.15), calls=%async_computation.3 | async-start | bytes 786432 | tf_op jit(solution)/shard_map/all_to_all | solution.py:1265
  167.3 0.0 copy-done.1
  167.3 3.7 %shard_map.279 = (f32[64,1024]{1,0:T(8,128)}, f32[3,64,1024]{2,1,0:T(8,128)}, f32[3,1024]{1,0:T(4,128)}, f32[16,256]{1,0:T(8,128)}) custom-call(s32[3]{0:T(128)} %pad_add_fusion.scalars, bf16[4,80,1024]{2,1,0:T(8,128)(2,1)} %copy-done.1, bf16[4,192,1024]{2,1,0:T(8,128)(2,1)} %copy-done, bf16[256,1024]{1,0:T(8,128)(2,1)} %features.7, ...), custom_call_target="tpu_custom_call" | custom-call | tf_op jit(solution)/shard_map/pallas_call | solution.py:1270
  171.0 0.7 convert.7
  171.7 7.1 %all-to-all-done.3 = bf16[8,96,256]{2,1,0:T(8,128)(2,1)S(1)} async-done(((bf16[8,96,256]{2,1,0:T(8,128)(2,1)}), bf16[8,96,256]{2,1,0:T(8,128)(2,1)S(1)}, u32[]{:S(2)}, u32[]{:S(2)}) %all-to-all-start.3) | async-done | bytes 393248 | tf_op jit(solution)/shard_map/all_to_all | solution.py:1265
  178.8 0.1 reduce
  179.0 16.2 %all_to_all.25.got = bf16[8,112,256]{2,1,0:T(8,128)(2,1)} all-to-all(bf16[8,112,256]{2,1,0:T(8,128)(2,1)S(1)} %broadcast_in_dim.2), channel_id=1, replica_groups=mesh['atoms'=8,'feat'=4] {'atoms'}, dimensions={0} | all-to-all | bytes 917504 | tf_op jit(solution)/shard_map/all_to_all | solution.py:1098
  195.2 2.0 %shard_map.280 = (f32[1,64]{1,0:T(1,128)}, f32[1,64]{1,0:T(1,128)}, f32[64,256]{1,0:T(8,128)}, f32[64,256]{1,0:T(8,128)}, f32[3,64,256]{2,1,0:T(8,128)}, /*index...) custom-call(bf16[8,112,256]{2,1,0:T(8,128)(2,1)} %all_to_all.25.got), custom_call_target="tpu_custom_call" | custom-call | tf_op jit(solution)/shard_map/pallas_call | solution.py:1287
  (3 shorter events, 0.1 us)
Async XLA Ops:
  3.3 13.8 %collective-permute-start = (bf16[352,128]{1,0:T(8,128)(2,1)}, bf16[352,128]{1,0:T(8,128)(2,1)S(1)}, u32[]{:S(2)}, u32[]{:S(2)}) collective-permute-start(bf16[352,128]{1,0:T(8,128)(2,1)} %get-tuple-element.62), channel_id=1, source_target_pairs={{0,4},{4,8},{8,12},{12,16},{16,20},{20,24},{24,28},{1,5},{5,9},{9,... | collective-permute-start | bytes 270344 | tf_op jit(solution)/shard_map/ppermute | solution.py:1125
  8.2 9.0 %collective-permute-start.1 = (bf16[352,128]{1,0:T(8,128)(2,1)}, bf16[352,128]{1,0:T(8,128)(2,1)S(1)}, u32[]{:S(2)}, u32[]{:S(2)}) collective-permute-start(bf16[352,128]{1,0:T(8,128)(2,1)} %get-tuple-element.63), channel_id=1, source_target_pairs={{4,0},{8,4},{12,8},{16,12},{20,16},{24,20},{28,24},{5,1},{9,5},{13... | collective-permute-start | bytes 270344 | tf_op jit(solution)/shard_map/ppermute | solution.py:1126
  9.5 7.1 %copy-start.6 = (bf16[3,64,64]{2,1,0:T(8,128)(2,1)S(1)}, bf16[3,64,64]{2,1,0:T(8,128)(2,1)}, u32[]{:S(2)}) copy-start(bf16[3,64,64]{2,1,0:T(8,128)(2,1)} %param.29) | copy-start | bytes 73732
  17.1 0.6 copy-start.4
  17.1 0.7 copy-start.5
  20.9 23.9 %all-to-all-start = ((bf16[4,64,1152]{2,1,0:T(8,128)(2,1)}), bf16[4,64,1152]{2,1,0:T(8,128)(2,1)S(1)}, u32[]{:S(2)}, u32[]{:S(2)}) async-start(bf16[4,64,1152]{2,1,0:T(8,128)(2,1)} %bitcast.27), calls=%async_computation | async-start | bytes 1179648 | tf_op jit(solution)/shard_map/all_to_all | solution.py:1166
  44.8 0.8 copy-start.3
  96.8 44.0 %all-to-all-start.1 = ((bf16[4,192,1024]{2,1,0:T(8,128)(2,1)}), bf16[4,192,1024]{2,1,0:T(8,128)(2,1)S(1)}, u32[]{:S(2)}, u32[]{:S(2)}) async-start(bf16[4,192,1024]{2,1,0:T(8,128)(2,1)} %get-tuple-element.75), calls=%async_computation.1 | async-start | bytes 3145728 | tf_op jit(solution)/shard_map/all_to_all | solution.py:1224
  140.9 5.7 %copy-start = (bf16[4,192,1024]{2,1,0:T(8,128)(2,1)}, bf16[4,192,1024]{2,1,0:T(8,128)(2,1)S(1)}, u32[]{:S(2)}) copy-start(bf16[4,192,1024]{2,1,0:T(8,128)(2,1)S(1)} %all-to-all-done.1.got_vec) | copy-start | bytes 4718596
  140.9 9.2 %copy-start.2 = (f32[608,256]{1,0:T(8,128)S(1)}, f32[608,256]{1,0:T(8,128)}, u32[]{:S(2)}) copy-start(f32[608,256]{1,0:T(8,128)} %get-tuple-element.92) | copy-start | bytes 1867780
  146.6 13.7 %all-to-all-start.2 = ((bf16[4,80,1024]{2,1,0:T(8,128)(2,1)}), bf16[4,80,1024]{2,1,0:T(8,128)(2,1)S(1)}, u32[]{:S(2)}, u32[]{:S(2)}) async-start(bf16[4,80,1024]{2,1,0:T(8,128)(2,1)} %get-tuple-element.86), calls=%async_computation.2 | async-start | bytes 1310720 | tf_op jit(solution)/shard_map/all_to_all | solution.py:1263
  160.3 7.0 %copy-start.1 = (bf16[4,80,1024]{2,1,0:T(8,128)(2,1)}, bf16[4,80,1024]{2,1,0:T(8,128)(2,1)S(1)}, u32[]{:S(2)}) copy-start(bf16[4,80,1024]{2,1,0:T(8,128)(2,1)S(1)} %all-to-all-done.2.got) | copy-start | bytes 1966084
  160.3 18.5 %all-to-all-start.3 = ((bf16[8,96,256]{2,1,0:T(8,128)(2,1)}), bf16[8,96,256]{2,1,0:T(8,128)(2,1)S(1)}, u32[]{:S(2)}, u32[]{:S(2)}) async-start(bf16[8,96,256]{2,1,0:T(8,128)(2,1)} %bitcast.15), calls=%async_computation.3 | async-start | bytes 786432 | tf_op jit(solution)/shard_map/all_to_all | solution.py:1265

commit v3 on v2

--- a/solution.py
+++ b/solution.py
@@ -192,6 +192,16 @@
         owned[at : at + width] = jnp.where((first >= 0) & (first < atoms), 1.0, 0.0)
 
 
+def set_picks(picks):
+    row = lax.broadcasted_iota(jnp.int32, (LANES, LANES), 0)
+    lane = lax.broadcasted_iota(jnp.int32, (LANES, LANES), 1)
+    base = jnp.where(lane >= R, R, 0)
+    for n in range(2 * OFFSETS):
+        which = 1 + n if n < OFFSETS else 33 + n - OFFSETS
+        block = jnp.where(row == base + which, 1.0, 0.0).astype(BF16)
+        picks[:, n * LANES : (n + 1) * LANES] = block
+
+
 def set_multiplicities(count, target, blocks, rows):
     lane = lax.broadcasted_iota(jnp.int32, (rows, LANES), 1)
     inner = jnp.where(lane >= R, lane - R, lane)
@@ -205,7 +215,7 @@
             value = jnp.where(inner == 32 + k, count[t + k], value)
         if t == SPAN - 1:
             value = jnp.where(doubled, 0.0, value)
-        target[t] = value
+        target[t] = value.astype(BF16)
 
 
 def dot(a, b):
@@ -227,7 +237,7 @@
 GEO_INVERSE, GEO_WAY = 0, 1
 
 
-def geometry(pos, many, t, rows, radial, geo, geo_s, geo_v):
+def geometry(pos, counts, t, rows, radial, geo, geo_s, geo_v):
     inv_space = (R - 1) / CUTOFF
 
     def step(k, _):
@@ -235,11 +245,12 @@
             here = pl.ds(pl.multiple_of(k * rows + o, SUB), size)
             part = slice(o, o + size)
             off = [p[t, part] - p[t + 1 + k, part] for p in pos]
-            close = many[t, part]
+            into = counts[part, pl.ds(pl.multiple_of(k * LANES, LANES), LANES)]
+            at = pl.multiple_of((OFFSETS + k) * LANES, LANES)
+            out_of = counts[part, pl.ds(at, LANES)]
             lane = lax.broadcasted_iota(jnp.int32, (size, LANES), 1)
             base = jnp.where(lane >= R, R, 0)
             centre = (lane - base).astype(F32)
-            near = base + (k + 1)
             square = off[0] * off[0] + off[1] * off[1] + off[2] * off[2]
             clamped = jnp.maximum(square, 0.01)
             inverse = lax.rsqrt(clamped)
@@ -264,8 +275,6 @@
                 geo_v[GEO_WAY + d, here, :] = (off[d] * inverse).astype(BF16)
             signed = jnp.where(square > 0.01, inverse, -inverse)
             geo_v[GEO_INVERSE, here, :] = signed.astype(BF16)
-            into = jnp.take_along_axis(close, near, axis=1)
-            out_of = jnp.take_along_axis(close, near + 32, axis=1)
             geo[GEO_INTO, here, :] = into.astype(BF16)
             geo[GEO_FROM, here, :] = out_of.astype(BF16)
         return 0
@@ -329,7 +338,7 @@
 def geometry_kernel(
     molecules, rows, atoms,
     scalars, own_count, own_pos, halo_ref, radial_out, geo_out, geo_s_out, geo_v_out,
-    near, near_last, px, py, pz, many, count, all_pos, all_count,
+    near, near_last, px, py, pz, many, count, all_pos, all_count, picks, counts,
 ):
     t = pl.program_id(0)
     start = scalars[0]
@@ -345,9 +354,11 @@
         extra = position_spreader(all_pos, (px, py, pz))
         spread(all_count, (None, count), blocks, distances, start, extra)
         set_multiplicities(count, many, blocks, rows)
-
+        set_picks(picks)
+
+    counts[...] = dot(many[t], picks[...])
     outs = [ref.at[0] for ref in (radial_out, geo_out, geo_s_out, geo_v_out)]
-    geometry((px, py, pz), many, t, rows, *outs)
+    geometry((px, py, pz), counts, t, rows, *outs)
 
 
 def vector_kernel(
@@ -666,7 +677,9 @@
     blocks = block_list(molecules, rows)
     return {
         "weights": ((2 * LANES, 2 * LANES), BF16),
-        "many": ((SPAN, rows, LANES), F32),
+        "many": ((SPAN, rows, LANES), BF16),
+        "picks": ((LANES, 2 * OFFSETS * LANES), BF16),
+        "counts": ((rows, 2 * OFFSETS * LANES), F32),
         "mask": ((rows, LANES), F32),
         "near": ((LANE_GROUPS, STEPS * blocks[0][1], WINDOW), jnp.int32),
         "near_last": ((LANE_GROUPS, STEPS * blocks[-1][1], WINDOW), jnp.int32),
@@ -1168,6 +1181,7 @@
     kinds = shared_scratch(atoms)
     batch = OFFSETS * rows_each
     names = ["near", "near_last"] + ["tall"] * 3 + ["many", "tall", "row1", "row1"]
+    names += ["picks", "counts"]
     radial, geo, geo_s, geo_v = edge_call(
         geometry_kernel,
         atoms,

time: 198 us -> 194 us (0.980)
  Pallas kernels: 126 us -> 122 us
    pallas_call x3, Pallas kernels: 95.4 us -> 91.6 us  [edge_call(): pl.pallas_call(functools.partial(kernel, molecules, rows, atoms), grid=(S...]
  transfers between devices with their start and end apart: 6 -> 6, of which waited for: 2 -> 2; matrix products, arithmetic and copies ran while one was open for 2% -> 2% of each run, Pallas kernels for 36% -> 35%
where the time goes in v3:
time: 194 us; the launch traced here: 193 us
  Pallas kernels  122 us (63%)
  blocking collectives  25.7 us (13%)
  starting transfers between devices  23.8 us (12%)
  waiting for transfers between devices  15.6 us (8%)
  other arithmetic  3.07 us (2%)
  local copies, waits for them, and re-layouts  2.13 us (1%)
    pallas_call x3, Pallas kernels, edge_call(): pl.pallas_call(functools.partial(kernel, molecules, rows, atoms), grid=(S...  91.6 us
    all_to_all x1, blocking collectives, everywhere(): lax.all_to_all(jnp.broadcast_to(x[None], (count,) + x.shape), axis, 0, 0)  16.2 us
    all_gather x1, blocking collectives, per_device(): gathered = lax.all_gather(scalar_sum, 'feat', axis=0, tiled=True)  9.48 us
    all_to_all x1, waiting for transfers between devices, per_device(): got = lax.all_to_all(send, 'feat', 0, 0)  8.5 us
    all_to_all x1, waiting for transfers between devices, per_device(): shares = lax.all_to_all(flat.reshape(count, share, H), 'atoms', 0, 0)  7.12 us
    pallas_call x1, Pallas kernels, per_device(): pl.pallas_call(functools.partial(layer_kernel, atoms), out_shape=[jax.Sha...  7.06 us
    pallas_call x1, Pallas kernels, per_device(): pl.pallas_call(functools.partial(dense_kernel, atoms), out_shape=[jax.Sha...  7.04 us
    all_to_all x1, starting transfers between devices, per_device(): shares = lax.all_to_all(flat.reshape(count, share, H), 'atoms', 0, 0)  6.96 us
  transfers between devices with their start and end apart: 6, of which 2 were waited for; matrix products, arithmetic and copies ran while one was open for 2% of the time, Pallas kernels for 35%

profile of v3, /device:TPU:0, one launch (start us, length us, event | category | flops | bytes accessed | tf_op | source)
XLA Modules:
  0.0 193.3 jit_solution(16445012127398697660)
XLA Ops:
  0.7 0.6 pad_add_fusion.scalars
  1.2 2.1 %shard_map.272 = (bf16[352,128]{1,0:T(8,128)(2,1)}, bf16[352,128]{1,0:T(8,128)(2,1)}) custom-call(s32[3]{0:T(128)} %pad_add_fusion.scalars, bf16[256,1024]{1,0:T(8,128)(2,1)} %features.7, bf16[3,256,1024]{2,1,0:T(8,128)(2,1)} %vectors.5, bf16[64,1024]{1,0:T(8,128)(2,1)} %cot_f.5, bf16[3,64,1024]{2,1,0:T(8,128)(2,1)} %cot_v.5, s32[32,1024]{1,0:T(8,128)} %refs_11_.1, ...), custom_call_target="tpu_custom_call" | custom-call | tf_op jit(solution)/shard_map/pallas_call | solution.py:751
  3.3 4.8 %collective-permute-start = (bf16[352,128]{1,0:T(8,128)(2,1)}, bf16[352,128]{1,0:T(8,128)(2,1)S(1)}, u32[]{:S(2)}, u32[]{:S(2)}) collective-permute-start(bf16[352,128]{1,0:T(8,128)(2,1)} %get-tuple-element.62), channel_id=1, source_target_pairs={{0,4},{4,8},{8,12},{12,16},{16,20},{20,24},{24,28},{1,5},{5,9},{9,... | collective-permute-start | bytes 270344 | tf_op jit(solution)/shard_map/ppermute | solution.py:1138
  8.2 1.3 collective-permute-start.1
  9.5 0.0 copy-start.6
  9.5 7.0 %shard_map.271 = (bf16[1024,1280]{1,0:T(8,128)(2,1)}, bf16[256,1024]{1,0:T(8,128)(2,1)}, f32[8,1024]{1,0:T(8,128)}) custom-call(s32[3]{0:T(128)} %pad_add_fusion.scalars, bf16[256,1024]{1,0:T(8,128)(2,1)} %features.7, bf16[3,256,1024]{2,1,0:T(8,128)(2,1)} %vectors.5, bf16[64,1024]{1,0:T(8,128)(2,1)} %cot_f.5, bf16[3,64,1024]{2,1,0:T(8,128)(2,1)} %cot_v.5, ...), custom_call_target="tpu_custom_call" | custom-call | flops 6000000000 | bytes 20000000 | tf_op jit(solution)/shard_map/pallas_call | solution.py:1152
  16.5 0.0 copy-done.6
  16.5 0.6 slice_bitcast_fusion
  17.1 0.0 collective-permute-done.low_ref
  17.1 0.0 copy-start.4
  17.1 0.0 collective-permute-done.1.high_ref
  17.1 0.0 copy-start.5
  17.2 0.6 copy-done.4
  17.8 0.0 copy-done.5
  17.8 3.1 %shard_map.273 = (bf16[128,1280]{1,0:T(8,128)(2,1)}, bf16[256,1152]{1,0:T(8,128)(2,1)}) custom-call(s32[3]{0:T(128)} %pad_add_fusion.scalars, bf16[352,128]{1,0:T(8,128)(2,1)} %copy-done.4, bf16[352,128]{1,0:T(8,128)(2,1)} %copy-done.5, bf16[256,1024]{1,0:T(8,128)(2,1)} %get-tuple-element.64.part_in, f32[1,256]{1,0:T(1,128)} %bitcast.49, f32[1,256]{1,0:T(1,128)} %bitcast.54, ...), custom_call_target="tpu_custom_call" | custom-call | tf_op jit(solution)/shard_map/pallas_call | solution.py:1168
  20.9 3.5 %all-to-all-start = ((bf16[4,64,1152]{2,1,0:T(8,128)(2,1)}), bf16[4,64,1152]{2,1,0:T(8,128)(2,1)S(1)}, u32[]{:S(2)}, u32[]{:S(2)}) async-start(bf16[4,64,1152]{2,1,0:T(8,128)(2,1)} %bitcast.27), calls=%async_computation | async-start | bytes 1179648 | tf_op jit(solution)/shard_map/all_to_all | solution.py:1179
  24.4 16.6 %shard_map.274 = (bf16[5,1568,256]{2,1,0:T(8,128)(2,1)}, bf16[5,3,1568,128]{3,2,1,0:T(8,128)(2,1)}, bf16[5,2,1568,128]{3,2,1,0:T(8,128)(2,1)}, bf16[5,4,1568,128]{3,2,1,0:T(8,128)(2,1)}) custom-call(s32[3]{0:T(128)} %pad_add_fusion.scalars, bf16[1024,1280]{1,0:T(8,128)(2,1)} %get-tuple-element.78.own_count.own_pos.own_ref, ...), custom_call_target="tpu_custom_call" | custom-call | flops 20000000000 | bytes 40000000 | tf_op jit(solution)/shard_map/pallas_call | solution.py:657
  41.0 0.0 all-to-all-done.scalar_parts
  41.0 0.0 copy-start.3
  41.0 0.8 copy-done.3
  41.8 34.7 %shard_map.275 = (bf16[64,1024]{1,0:T(8,128)(2,1)}, bf16[192,1024]{1,0:T(8,128)(2,1)}, f32[128,256]{1,0:T(8,128)}, bf16[5,1568,128]{2,1,0:T(8,128)(2,1)}) custom-call(s32[3]{0:T(128)} %pad_add_fusion.scalars, bf16[1024,1280]{1,0:T(8,128)(2,1)} %get-tuple-element.78.own_count.own_pos.own_ref, bf16[128,1280]{1,0:T(8,128)(2,1)} %get-tuple-element.65.halo_ref, ...), custom_call_target="tpu_custom_call" | custom-call | flops 20000000000 | bytes 40000000 | tf_op jit(solution)/shard_map/pallas_call | solution.py:657
  76.5 9.5 %all_gather.3.gathered = bf16[256,1024]{1,0:T(8,128)(2,1)} all-gather(bf16[64,1024]{1,0:T(8,128)(2,1)} %get-tuple-element.70), channel_id=1, replica_groups=mesh['atoms'=8,'feat'=4] {'feat'}, dimensions={0}, use_global_device_ids=true | all-gather | bytes 655360 | tf_op jit(solution)/shard_map/all_gather | solution.py:1213
  86.0 7.1 %shard_map.276 = (bf16[64,1024]{1,0:T(8,128)(2,1)}, f32[3,64,1024]{2,1,0:T(8,128)}, f32[8,1024]{1,0:T(8,128)}, bf16[4,192,1024]{2,1,0:T(8,128)(2,1)}, f32[608,256]{1,0:T(8,128)}) custom-call(s32[3]{0:T(128)} %pad_add_fusion.scalars, bf16[256,1024]{1,0:T(8,128)(2,1)} %features.7, f32[8,1024]{1,0:T(8,128)} %get-tuple-element.60.stat, ...), custom_call_target="tpu_custom_call" | custom-call | tf_op jit(solution)/shard_map/pallas_call | solution.py:1219
  93.0 3.7 %all-to-all-start.1 = ((bf16[4,192,1024]{2,1,0:T(8,128)(2,1)}), bf16[4,192,1024]{2,1,0:T(8,128)(2,1)S(1)}, u32[]{:S(2)}, u32[]{:S(2)}) async-start(bf16[4,192,1024]{2,1,0:T(8,128)(2,1)} %get-tuple-element.75), calls=%async_computation.1 | async-start | bytes 3145728 | tf_op jit(solution)/shard_map/all_to_all | solution.py:1238
  96.8 40.3 %shard_map.277 = (f32[3,64,1024]{2,1,0:T(8,128)}, f32[3,64,1024]{2,1,0:T(8,128)}, bf16[128,1024]{1,0:T(8,128)(2,1)}, f32[8,1024]{1,0:T(8,128)}, f32[128,256]{1,0:T(8,128)}) custom-call(s32[3]{0:T(128)} %pad_add_fusion.scalars, bf16[1024,1280]{1,0:T(8,128)(2,1)} %get-tuple-element.78.own_count.own_pos.own_ref, bf16[128,1280]{1,0:T(8,128)(2,1)} %get-tuple-element.65.halo_ref, ...), custom_call_target="tpu_custom_call" | custom-call | flops 20000000000 | bytes 40000000 | tf_op jit(solution)/shard_map/pallas_call | solution.py:657
  137.1 0.0 all-to-all-done.1.got_vec
  137.1 0.0 copy-start
  137.1 0.0 copy-start.2
  137.1 5.7 %shard_map.278 = (bf16[3,64,1024]{2,1,0:T(8,128)(2,1)}, bf16[4,80,1024]{2,1,0:T(8,128)(2,1)}, bf16[160,256]{1,0:T(8,128)(2,1)}) custom-call(s32[3]{0:T(128)} %pad_add_fusion.scalars, bf16[256,1024]{1,0:T(8,128)(2,1)} %features.7, f32[8,1024]{1,0:T(8,128)} %get-tuple-element.60.stat, bf16[3,256,1024]{2,1,0:T(8,128)(2,1)} %vectors.5, ...), custom_call_target="tpu_custom_call" | custom-call | tf_op jit(solution)/shard_map/pallas_call | solution.py:1265
  142.8 0.0 copy-done
  142.8 3.5 %all-to-all-start.2 = ((bf16[4,80,1024]{2,1,0:T(8,128)(2,1)}), bf16[4,80,1024]{2,1,0:T(8,128)(2,1)S(1)}, u32[]{:S(2)}, u32[]{:S(2)}) async-start(bf16[4,80,1024]{2,1,0:T(8,128)(2,1)} %get-tuple-element.86), calls=%async_computation.2 | async-start | bytes 1310720 | tf_op jit(solution)/shard_map/all_to_all | solution.py:1277
  146.3 0.0 copy-done.2
  146.4 1.7 pad_maximum_fusion
  148.0 8.5 %all-to-all-done.2.got = bf16[4,80,1024]{2,1,0:T(8,128)(2,1)S(1)} async-done(((bf16[4,80,1024]{2,1,0:T(8,128)(2,1)}), bf16[4,80,1024]{2,1,0:T(8,128)(2,1)S(1)}, u32[]{:S(2)}, u32[]{:S(2)}) %all-to-all-start.2) | async-done | bytes 655392 | tf_op jit(solution)/shard_map/all_to_all | solution.py:1277
  156.5 0.0 copy-start.1
  156.5 7.0 %all-to-all-start.3 = ((bf16[8,96,256]{2,1,0:T(8,128)(2,1)}), bf16[8,96,256]{2,1,0:T(8,128)(2,1)S(1)}, u32[]{:S(2)}, u32[]{:S(2)}) async-start(bf16[8,96,256]{2,1,0:T(8,128)(2,1)} %bitcast.15), calls=%async_computation.3 | async-start | bytes 786432 | tf_op jit(solution)/shard_map/all_to_all | solution.py:1279
  163.5 0.0 copy-done.1
  163.5 3.7 %shard_map.279 = (f32[64,1024]{1,0:T(8,128)}, f32[3,64,1024]{2,1,0:T(8,128)}, f32[3,1024]{1,0:T(4,128)}, f32[16,256]{1,0:T(8,128)}) custom-call(s32[3]{0:T(128)} %pad_add_fusion.scalars, bf16[4,80,1024]{2,1,0:T(8,128)(2,1)} %copy-done.1, bf16[4,192,1024]{2,1,0:T(8,128)(2,1)} %copy-done, bf16[256,1024]{1,0:T(8,128)(2,1)} %features.7, ...), custom_call_target="tpu_custom_call" | custom-call | tf_op jit(solution)/shard_map/pallas_call | solution.py:1284
  167.2 0.7 convert.7
  167.9 7.1 %all-to-all-done.3 = bf16[8,96,256]{2,1,0:T(8,128)(2,1)S(1)} async-done(((bf16[8,96,256]{2,1,0:T(8,128)(2,1)}), bf16[8,96,256]{2,1,0:T(8,128)(2,1)S(1)}, u32[]{:S(2)}, u32[]{:S(2)}) %all-to-all-start.3) | async-done | bytes 393248 | tf_op jit(solution)/shard_map/all_to_all | solution.py:1279
  175.0 0.1 reduce
  175.1 16.2 %all_to_all.25.got = bf16[8,112,256]{2,1,0:T(8,128)(2,1)} all-to-all(bf16[8,112,256]{2,1,0:T(8,128)(2,1)S(1)} %broadcast_in_dim.2), channel_id=1, replica_groups=mesh['atoms'=8,'feat'=4] {'atoms'}, dimensions={0} | all-to-all | bytes 917504 | tf_op jit(solution)/shard_map/all_to_all | solution.py:1111
  191.3 2.0 %shard_map.280 = (f32[1,64]{1,0:T(1,128)}, f32[1,64]{1,0:T(1,128)}, f32[64,256]{1,0:T(8,128)}, f32[64,256]{1,0:T(8,128)}, f32[3,64,256]{2,1,0:T(8,128)}, /*index...) custom-call(bf16[8,112,256]{2,1,0:T(8,128)(2,1)} %all_to_all.25.got), custom_call_target="tpu_custom_call" | custom-call | tf_op jit(solution)/shard_map/pallas_call | solution.py:1301
  (3 shorter events, 0.1 us)
Async XLA Ops:
  3.3 13.8 %collective-permute-start = (bf16[352,128]{1,0:T(8,128)(2,1)}, bf16[352,128]{1,0:T(8,128)(2,1)S(1)}, u32[]{:S(2)}, u32[]{:S(2)}) collective-permute-start(bf16[352,128]{1,0:T(8,128)(2,1)} %get-tuple-element.62), channel_id=1, source_target_pairs={{0,4},{4,8},{8,12},{12,16},{16,20},{20,24},{24,28},{1,5},{5,9},{9,... | collective-permute-start | bytes 270344 | tf_op jit(solution)/shard_map/ppermute | solution.py:1138
  8.2 9.0 %collective-permute-start.1 = (bf16[352,128]{1,0:T(8,128)(2,1)}, bf16[352,128]{1,0:T(8,128)(2,1)S(1)}, u32[]{:S(2)}, u32[]{:S(2)}) collective-permute-start(bf16[352,128]{1,0:T(8,128)(2,1)} %get-tuple-element.63), channel_id=1, source_target_pairs={{4,0},{8,4},{12,8},{16,12},{20,16},{24,20},{28,24},{5,1},{9,5},{13... | collective-permute-start | bytes 270344 | tf_op jit(solution)/shard_map/ppermute | solution.py:1139
  9.5 7.1 %copy-start.6 = (bf16[3,64,64]{2,1,0:T(8,128)(2,1)S(1)}, bf16[3,64,64]{2,1,0:T(8,128)(2,1)}, u32[]{:S(2)}) copy-start(bf16[3,64,64]{2,1,0:T(8,128)(2,1)} %param.29) | copy-start | bytes 73732
  17.1 0.6 copy-start.4
  17.1 0.7 copy-start.5
  20.9 20.1 %all-to-all-start = ((bf16[4,64,1152]{2,1,0:T(8,128)(2,1)}), bf16[4,64,1152]{2,1,0:T(8,128)(2,1)S(1)}, u32[]{:S(2)}, u32[]{:S(2)}) async-start(bf16[4,64,1152]{2,1,0:T(8,128)(2,1)} %bitcast.27), calls=%async_computation | async-start | bytes 1179648 | tf_op jit(solution)/shard_map/all_to_all | solution.py:1179
  41.0 0.8 copy-start.3
  93.0 44.0 %all-to-all-start.1 = ((bf16[4,192,1024]{2,1,0:T(8,128)(2,1)}), bf16[4,192,1024]{2,1,0:T(8,128)(2,1)S(1)}, u32[]{:S(2)}, u32[]{:S(2)}) async-start(bf16[4,192,1024]{2,1,0:T(8,128)(2,1)} %get-tuple-element.75), calls=%async_computation.1 | async-start | bytes 3145728 | tf_op jit(solution)/shard_map/all_to_all | solution.py:1238
  137.1 5.7 %copy-start = (bf16[4,192,1024]{2,1,0:T(8,128)(2,1)}, bf16[4,192,1024]{2,1,0:T(8,128)(2,1)S(1)}, u32[]{:S(2)}) copy-start(bf16[4,192,1024]{2,1,0:T(8,128)(2,1)S(1)} %all-to-all-done.1.got_vec) | copy-start | bytes 4718596
  137.1 9.2 %copy-start.2 = (f32[608,256]{1,0:T(8,128)S(1)}, f32[608,256]{1,0:T(8,128)}, u32[]{:S(2)}) copy-start(f32[608,256]{1,0:T(8,128)} %get-tuple-element.92) | copy-start | bytes 1867780
  142.8 13.7 %all-to-all-start.2 = ((bf16[4,80,1024]{2,1,0:T(8,128)(2,1)}), bf16[4,80,1024]{2,1,0:T(8,128)(2,1)S(1)}, u32[]{:S(2)}, u32[]{:S(2)}) async-start(bf16[4,80,1024]{2,1,0:T(8,128)(2,1)} %get-tuple-element.86), calls=%async_computation.2 | async-start | bytes 1310720 | tf_op jit(solution)/shard_map/all_to_all | solution.py:1277
  156.5 7.0 %copy-start.1 = (bf16[4,80,1024]{2,1,0:T(8,128)(2,1)}, bf16[4,80,1024]{2,1,0:T(8,128)(2,1)S(1)}, u32[]{:S(2)}) copy-start(bf16[4,80,1024]{2,1,0:T(8,128)(2,1)S(1)} %all-to-all-done.2.got) | copy-start | bytes 1966084
  156.5 18.5 %all-to-all-start.3 = ((bf16[8,96,256]{2,1,0:T(8,128)(2,1)}), bf16[8,96,256]{2,1,0:T(8,128)(2,1)S(1)}, u32[]{:S(2)}, u32[]{:S(2)}) async-start(bf16[8,96,256]{2,1,0:T(8,128)(2,1)} %bitcast.15), calls=%async_computation.3 | async-start | bytes 786432 | tf_op jit(solution)/shard_map/all_to_all | solution.py:1279
